TPU v7x, 256 devices: a whole 4x4x8 slice. The times are simulated.
256 devices in a mesh: dp: 16 (over x_lo, z), tensor: 16 (over y, x_hi, core).
Axes of the slice: x: 4 (x_hi: 2, x_lo: 2; x = x_hi * 2 + x_lo), y: 4, z: 8, core: 2. Of those that a mesh axis runs over, the one named last changes fastest.
Arguments:
- attention: bfloat16 [4096, 8192], P('dp', 'tensor'), may hold values from -6 to 6
- output_weight_frozen: bfloat16 [8192, 16384], P('dp', 'tensor'), may hold values from -0.0625 to 0.0625
- residual: bfloat16 [4096, 16384], P('dp', 'tensor'), may hold values from -40 to 40
- cotangent: bfloat16 [4, 4096, 16384], P(None, 'dp', 'tensor'), may hold values from -1 to 1
- output_norm_scale: float32 [16384], P('tensor'), may hold values from 0.5 to 1.5
- adapter_down_weights: bfloat16 [4, 64, 8192], replicated, may hold values from -0.0625 to 0.0625
- adapter_up_weights: bfloat16 [4, 64, 16384], P(None, None, 'tensor'), may hold values from -0.625 to 0.625
- objective: int32 [4], replicated, may hold values from 0 to 3
Outputs:
- fisher_a: float32 [4, 64, 8192], P(None, 'dp', 'tensor')
- fisher_b: float32 [4, 64, 16384], P(None, 'dp', 'tensor')
All inputs are finite; a program needn't handle non-finite values.
Results may differ from a plain program's by a relative error of at most 0.0015.
Values may be sent and summed in bfloat16 or wider, within the bound.
A program may use at most 128 MiB of HBM per device.

v0:
```python
import jax
import jax.numpy as jnp
from jax import lax
from jax.sharding import PartitionSpec as P

MODEL_WIDTH = 16384
ADAPTER_RANK = 64
ADAPTER_COUNT = 4
PASSES = 4
LEN = 256


epsilon = 1e-05


def body(
    attention,
    output_weight_frozen,
    residual,
    cotangent,
    output_norm_scale,
    adapter_down_weights,
    adapter_up_weights,
    objective,
):
    tokens_here = attention.shape[0]
    columns = output_weight_frozen.shape[1]
    features_here = attention.shape[1]
    examples_here = tokens_here // LEN
    examples_all = examples_here * lax.axis_size("dp")
    gathered = lax.all_gather(attention, "tensor", axis=1, tiled=True)
    base = jnp.dot(
        gathered,
        lax.all_gather(output_weight_frozen, "dp", axis=0, tiled=True),
        preferred_element_type=jnp.float32,
    )
    partial_sum = residual.astype(jnp.float32) + base
    selector_all = (
        objective[:, None] == jnp.arange(ADAPTER_COUNT, dtype=jnp.int32)[None, :]
    ).astype(jnp.float32)
    attn_split = attention.reshape(examples_here, LEN, features_here)
    rows_here = ADAPTER_RANK // lax.axis_size("dp")
    fisher_a = jnp.zeros((ADAPTER_COUNT, rows_here, features_here), jnp.float32)
    fisher_b = jnp.zeros((ADAPTER_COUNT, rows_here, columns), jnp.float32)
    for step in range(PASSES):
        last = step + 1
        adapter_picker = selector_all[step:last].astype(jnp.bfloat16)
        down_maps = jnp.einsum(
            "tf,fqb->tqb", adapter_picker, adapter_down_weights, preferred_element_type=jnp.float32
        ).astype(jnp.bfloat16)
        up_maps = jnp.einsum(
            "nj,jul->nul", adapter_picker, adapter_up_weights, preferred_element_type=jnp.float32
        ).astype(jnp.bfloat16)
        lowered = jnp.einsum(
            "th,prh->ptr", gathered, down_maps, preferred_element_type=jnp.float32
        ).astype(jnp.bfloat16)
        hidden_sum = partial_sum[None] + jnp.einsum(
            "ptr,prd->ptd", lowered, up_maps, preferred_element_type=jnp.float32
        )
        weighted = cotangent[step:last].astype(jnp.float32) * output_norm_scale
        squares, inner = lax.psum(
            (jnp.sum(hidden_sum * hidden_sum, axis=-1), jnp.sum(weighted * hidden_sum, axis=-1)),
            "tensor",
        )
        scale_inv = lax.rsqrt(squares / MODEL_WIDTH + epsilon)[..., None]
        grad_out = (
            scale_inv * weighted - hidden_sum * inner[..., None] * scale_inv**3 / MODEL_WIDTH
        ).astype(jnp.bfloat16)
        low_terms = jnp.einsum(
            "ptd,prd->ptr", grad_out, up_maps, preferred_element_type=jnp.float32
        )
        grad_low = lax.psum(low_terms, "tensor").astype(jnp.bfloat16)
        count = last - step
        per_b = jnp.einsum(
            "pelr,peld->perd",
            lowered.reshape(count, examples_here, LEN, ADAPTER_RANK),
            grad_out.reshape(count, examples_here, LEN, columns),
            preferred_element_type=jnp.float32,
        )
        per_a = jnp.einsum(
            "pelr,pelh->perh",
            grad_low.reshape(count, examples_here, LEN, ADAPTER_RANK),
            attn_split[None],
            preferred_element_type=jnp.float32,
        )
        square_a = jnp.sum(per_a * per_a, axis=1)
        square_b = jnp.sum(per_b * per_b, axis=1)
        owned_a = lax.psum_scatter(square_a, "dp", scatter_dimension=1, tiled=True)
        owned_b = lax.psum_scatter(square_b, "dp", scatter_dimension=1, tiled=True)
        fisher_a = fisher_a + selector_all[step][:, None, None] * owned_a
        fisher_b = fisher_b + selector_all[step][:, None, None] * owned_b
    return (fisher_a / examples_all, fisher_b / examples_all)


def solution(mesh):
    placed = (
        P("dp", "tensor"),
        P("dp", "tensor"),
        P("dp", "tensor"),
        P(None, "dp", "tensor"),
        P("tensor"),
        P(),
        P(None, None, "tensor"),
        P(),
    )
    return jax.shard_map(
        body,
        mesh=mesh,
        in_specs=placed,
        out_specs=(P(None, "dp", "tensor"), P(None, "dp", "tensor")),
        check_vma=False,
    )
```

profile of v0, /device:TPU:1, one launch (start us, length us, event | category | flops | bytes accessed | tf_op | source)
XLA Modules:
  0.0 537.7 jit_solution(212172281559871555)
XLA Ops:
  7.2 0.7 all-gather.3.cloned.1.call-update
  8.0 0.7 all-gather.5.cloned.1.call-update
  8.7 0.9 fusion.48
  9.6 1.2 fusion.32
  10.8 0.5 fusion.34
  11.8 0.5 fusion.38
  12.3 4.0 fusion.6
  16.4 5.1 fusion.4
  21.5 5.1 fusion.2
  26.6 5.1 fusion
  31.7 45.0 %all-gather.3.cloned.1.call-done = bf16[256,8192]{1,0:T(8,128)(2,1)} async-done(((bf16[256,512]{1,0:T(8,128)(2,1)}), bf16[256,8192]{1,0:T(8,128)(2,1)}) %all-gather.3.cloned.1.call-update) | async-done | bytes 4194320 | tf_op jit(solution)/shard_map/all_gather | solution.py:31
  76.7 4.7 fusion.19
  81.4 3.5 fusion.18
  84.9 1.8 fusion.17
  86.7 1.9 fusion.16
  88.6 172.5 %all-gather.5.cloned.1.call-done = bf16[8192,1024]{1,0:T(8,128)(2,1)} async-done(((bf16[512,1024]{1,0:T(8,128)(2,1)}), bf16[8192,1024]{1,0:T(8,128)(2,1)}) %all-gather.5.cloned.1.call-update) | async-done | bytes 16777232 | tf_op jit(solution)/shard_map/all_gather | solution.py:34
  261.1 11.5 %convolution_add_fusion = f32[256,1024]{1,0:T(8,128)S(1)} fusion(bf16[256,8192]{1,0:T(8,128)(2,1)} %all-gather.3.cloned.1.call-done, bf16[8192,1024]{1,0:T(8,128)(2,1)} %all-gather.5.cloned.1.call-done, bf16[256,1024]{1,0:T(8,128)(2,1)} %param.10), kind=kOutput, calls=%fused_computation.4 | convolution fusion | flops 4295491584 | bytes 22544384 | tf_op jit(solution)/shard_map/dot_general | solution.py:32
  273.4 1.0 multiply_reduce_fusion.2
  274.4 3.5 fusion.27
  277.9 1.0 copy-done.4
  279.0 0.7 multiply_reduce_fusion.3
  279.7 34.4 %all-reduce.9 = (f32[1,256]{1,0:T(1,128)}, f32[256]{0:T(256)}, f32[1,256]{1,0:T(1,128)}, f32[256]{0:T(256)}, f32[1,256]{1,0:T(1,128)}, /*index=5*/f32[256]{0:T(256)}, f32[1,256]{1,0:T(1,128)}, f32[256]{0:T(256)}) all-reduce(f32[1,256]{1,0:T(1,128)S(1)} %bitcast.255, ...), channel_id=1, replica_groups=mesh['dp'=16,'tensor'=16] {'tensor'}, use_global_device_ids=true, to_apply=%region_19.0 | all-reduce | flops 2048 | bytes 16384 | tf_op jit(solution)/shard_map/psum | solution.py:61
  314.1 0.8 add_rsqrt_fusion
  314.9 1.4 fusion.31
  316.3 1.2 convolution_bitcast_fusion
  317.5 1.0 fusion.11
  318.5 0.7 add_rsqrt_fusion.2
  319.2 2.2 fusion.28
  321.7 0.9 fusion.10
  322.9 0.9 fusion.9
  324.1 0.9 fusion.8
  325.1 66.4 %all-reduce.15 = (bf16[1,256,64]{1,2,0:T(8,128)(2,1)S(1)}, bf16[1,256,64]{1,2,0:T(8,128)(2,1)S(1)}, bf16[1,256,64]{1,2,0:T(8,128)(2,1)S(1)}, bf16[1,256,64]{1,2,0:T(8,128)(2,1)S(1)}) all-reduce(f32[1,256,64]{1,2,0:T(8,128)S(1)} %convolution_bitcast_fusion, ...), channel_id=1, replica_groups=mesh['dp'=16,'tensor'=16] {'tensor'}, use_global_device_ids=true, to_apply=%region_22.0 | all-reduce | flops 65536 | bytes 393216 | tf_op jit(solution)/shard_map/psum | solution.py:72
  391.5 0.8 fusion.15
  392.3 0.8 fusion.14
  393.1 0.8 fusion.13
  393.9 0.8 fusion.12
  394.8 0.6 dynamic-slice
  396.0 127.7 %all-reduce.14.cloned.1.call-done = (f32[1,64,512]{2,1,0:T(8,128)}, f32[1,64,512]{2,1,0:T(8,128)}, f32[1,64,512]{2,1,0:T(8,128)}, f32[1,64,512]{2,1,0:T(8,128)},...) async-done(((f32[1,64,512]{2,1,0:T(8,128)}, f32[1,64,512]{2,1,0:T(8,128)}, f32[1,64,512]{2,1,0:T(8,128)}, ...) | async-done | bytes 1572880
  523.7 0.7 dynamic-slice_bitcast_fusion.4
  524.5 0.7 dynamic-slice_bitcast_fusion.5
  525.2 0.7 dynamic-slice_bitcast_fusion.6
  525.9 0.7 dynamic-slice_bitcast_fusion.7
  526.6 0.8 dynamic-slice_bitcast_fusion
  527.4 0.8 dynamic-slice_bitcast_fusion.1
  528.2 0.8 dynamic-slice_bitcast_fusion.2
  528.9 0.8 dynamic-slice_bitcast_fusion.3
  529.7 0.7 add_multiply_fusion.1
  530.4 0.7 add_multiply_fusion
  (38 shorter events, 2.4 us)
Async XLA Ops:
  7.2 2.4 copy-start
  7.2 69.5 %all-gather.3.cloned.1.call-start = ((), (), s32[]{:S(2)}) async-start(), calls=%async_computation | async-start | bytes 4456448 | tf_op jit(solution)/shard_map/all_gather | solution.py:31
  7.9 253.2 %all-gather.5.cloned.1.call-start = ((), (), s32[]{:S(2)}) async-start(), calls=%async_computation.1 | async-start | bytes 17825792 | tf_op jit(solution)/shard_map/all_gather | solution.py:34
  8.7 515.1 %all-reduce.14.cloned.1.call-start = ((), (), s32[]{:S(2)}) async-start(), calls=%async_computation.2 | async-start | bytes 3145728
  8.7 3.6 copy-start.10
  76.7 4.8 copy-start.1
  76.7 8.2 %copy-start.7 = (bf16[1,64,8192]{2,0,1:T(2,128)(2,1)S(1)}, bf16[1,64,8192]{2,0,1:T(2,128)(2,1)}, u32[]{:S(2)}) copy-start(bf16[1,64,8192]{2,0,1:T(2,128)(2,1)} %fusion.4) | copy-start | bytes 3145732
  88.6 184.1 %copy-start.8 = (bf16[1,64,1024]{2,0,1:T(2,128)(2,1)S(1)}, bf16[1,64,1024]{2,0,1:T(2,128)(2,1)}, u32[]{:S(2)}) copy-start(bf16[1,64,1024]{2,0,1:T(2,128)(2,1)} %fusion.32) | copy-start | bytes 393220
  272.6 1.8 copy-start.9
  274.4 3.5 copy-start.2
  277.9 1.0 copy-start.4
  314.1 5.1 copy-start.3
  314.1 5.1 copy-start.5
  319.2 72.2 %copy-start.6 = (bf16[256,512]{1,0:T(8,128)(2,1)S(1)}, bf16[256,512]{1,0:T(8,128)(2,1)}, u32[]{:S(2)}) copy-start(bf16[256,512]{1,0:T(8,128)(2,1)} %param.8) | copy-start | bytes 786436
  321.4 73.4 %copy-start.11 = (u32[256]{0:T(256)S(1)}, u32[256]{0:T(256)}, u32[]{:S(2)}) copy-start(u32[256]{0:T(256)} %constant.22) | copy-start | bytes 3076
Sparse Core Ops, SparseCore 0:
  10.6 65.9 all-gather.2
  78.4 182.6 all-gather.4
  394.9 128.8 all-reduce.13
where the time goes:
time: 548 us; the launch traced here: 538 us
  waiting for transfers between devices  347 us (63%)
  blocking collectives  101 us (18%)
  matrix products  59.8 us (11%)
  between operations  14.7 us (3%)
  other arithmetic  8.09 us (1%)
  local copies, waits for them, and re-layouts  7.62 us (1%)
    all_gather x1, waiting for transfers between devices, body(): lax.all_gather(output_weight_frozen, 'dp', axis=0, tiled=True)  173 us
    unnamed x4, waiting for transfers between devices  129 us
    psum x1, blocking collectives, body(): grad_low = lax.psum(low_terms, 'tensor').astype(jnp.bfloat16)  66.4 us
    all_gather x1, waiting for transfers between devices, body(): gathered = lax.all_gather(attention, 'tensor', axis=1, tiled=True)  45 us
    psum x1, blocking collectives, body(): lax.psum((jnp.sum(hidden_sum * hidden_sum, axis=-1), jnp.sum(weighted * h...  34.4 us
    dot_general x4, matrix products, body(): jnp.einsum('tf,fqb->tqb', adapter_picker, adapter_down_weights, preferred...  19.3 us
    dot_general x4, matrix products, body(): jnp.einsum('th,prh->ptr', gathered, down_maps, preferred_element_type=jnp...  11.8 us
    dot_general x1, matrix products, body(): jnp.dot(gathered, lax.all_gather(output_weight_frozen, 'dp', axis=0, tile...  11.5 us
  transfers between devices with their start and end apart: 3, of which 3 were waited for; matrix products, arithmetic and copies ran while one was open for 7% of the time, Pallas kernels for 0%

commit v1 on v0

v1 whole, which is shorter than its diff:
```python
import jax
import jax.numpy as jnp
from jax import lax
from jax.experimental import pallas as pl
from jax.experimental.pallas import tpu as pltpu
from jax.sharding import PartitionSpec as P

MODEL_WIDTH = 16384
ADAPTER_RANK = 64
ADAPTER_COUNT = 4
PASSES = 4
LEN = 256
EXAMPLES = 16
GROUP = 16
MESH = pl.DeviceIdType.MESH

epsilon = 1e-05


def to_tensor(step):
    return (lax.axis_index("dp"), lax.rem(lax.axis_index("tensor") + step, GROUP))


def to_dp(step):
    return (lax.rem(lax.axis_index("dp") + step, GROUP), lax.axis_index("tensor"))


def each_other(action):
    def one(step, carry):
        action(step)
        return carry

    lax.fori_loop(1, GROUP, one, 0)


def spread_rows(step):
    per = ADAPTER_RANK // GROUP
    row = lax.broadcasted_iota(jnp.int32, (PASSES * ADAPTER_RANK, ADAPTER_RANK), 0)
    col = lax.broadcasted_iota(jnp.int32, (PASSES * ADAPTER_RANK, ADAPTER_RANK), 1)
    goal = (col // per) * (PASSES * per) + step * per + col % per
    return jnp.where(row == goal, 1.0, 0.0).astype(jnp.bfloat16)


def tail_kernel(
    objective,
    partial,
    low,
    cotangent,
    scale,
    up,
    attention,
    out_a,
    out_b,
    hidden,
    grads,
    low_wide,
    up_wide,
    stat_slots,
    low_terms,
    low_slots,
    grad_low,
    square_b,
    slots_b,
    square_a,
    slots_a,
    stat_send,
    stat_recv,
    term_send,
    term_recv,
    full_send,
    full_recv,
    b_send,
    b_recv,
    a_send,
    a_recv,
):
    me_d = lax.axis_index("dp")
    me_t = lax.axis_index("tensor")
    barrier = pltpu.get_barrier_semaphore()

    def greet(step):
        pl.semaphore_signal(barrier, inc=1, device_id=to_tensor(step), device_id_type=MESH)
        pl.semaphore_signal(barrier, inc=1, device_id=to_dp(step), device_id_type=MESH)

    each_other(greet)

    lane = lax.broadcasted_iota(jnp.int32, (LEN, 128), 1)
    stats = jnp.zeros((LEN, 128), jnp.float32)
    for step in range(PASSES):
        picked = objective[step]
        spread = spread_rows(step)
        low_wide[step] = lax.dot_general(
            low[picked], spread, (((1,), (1,)), ((), ())), preferred_element_type=jnp.float32
        ).astype(jnp.bfloat16)
        up_wide[step] = jnp.dot(
            spread, up[picked], preferred_element_type=jnp.float32
        ).astype(jnp.bfloat16)
        value = partial[...] + jnp.dot(
            low_wide[step], up_wide[step], preferred_element_type=jnp.float32
        )
        hidden[step] = value
        weighted = cotangent[step].astype(jnp.float32) * scale[...]
        squares = jnp.sum(value * value, axis=1, keepdims=True)
        inner = jnp.sum(weighted * value, axis=1, keepdims=True)
        stats = jnp.where(lane == 2 * step, squares, stats)
        stats = jnp.where(lane == 2 * step + 1, inner, stats)
    stat_slots[0] = stats.T[: 2 * PASSES]

    pl.semaphore_wait(barrier, 2 * (GROUP - 1))

    def stat_copy(step):
        return pltpu.make_async_remote_copy(
            src_ref=stat_slots.at[0],
            dst_ref=stat_slots.at[step],
            send_sem=stat_send.at[step],
            recv_sem=stat_recv.at[step],
            device_id=to_tensor(step),
            device_id_type=MESH,
        )

    each_other(lambda step: stat_copy(step).start())
    each_other(lambda step: stat_copy(step).wait())
    totals = jnp.sum(stat_slots[...], axis=0)
    kinds = lax.broadcasted_iota(jnp.int32, totals.shape, 0)
    inner_first = jnp.concatenate([totals[1:], totals[:1]], axis=0)
    scale_inv = lax.rsqrt(totals / MODEL_WIDTH + epsilon)
    weight_hidden = inner_first * scale_inv**3 / MODEL_WIDTH
    keep = jnp.concatenate(
        [scale_inv, weight_hidden, jnp.zeros((128 - 4 * PASSES, LEN), jnp.float32)], axis=0
    )
    keep = jnp.where(
        lax.broadcasted_iota(jnp.int32, keep.shape, 0) % 2 == 0, keep, 0.0
    )
    columns = keep.T

    terms = None
    for step in range(PASSES):
        weighted = cotangent[step].astype(jnp.float32) * scale[...]
        per_token = columns[:, 2 * step : 2 * step + 1]
        back = columns[:, 2 * PASSES + 2 * step : 2 * PASSES + 2 * step + 1]
        grads[step] = (per_token * weighted - hidden[step] * back).astype(jnp.bfloat16)
        term = lax.dot_general(
            grads[step], up_wide[step], (((1,), (1,)), ((), ())), preferred_element_type=jnp.float32
        )
        terms = term if terms is None else terms + term
    low_terms[...] = terms.reshape(low_terms.shape)

    def term_copy(step):
        return pltpu.make_async_remote_copy(
            src_ref=low_terms.at[lax.rem(me_t + step, GROUP)],
            dst_ref=low_slots.at[step],
            send_sem=term_send.at[step],
            recv_sem=term_recv.at[step],
            device_id=to_tensor(step),
            device_id_type=MESH,
        )

    each_other(lambda step: term_copy(step).start())

    per_b = None
    for step in range(PASSES):
        term = lax.dot_general(
            low_wide[step], grads[step], (((0,), (0,)), ((), ())), preferred_element_type=jnp.float32
        )
        per_b = term if per_b is None else per_b + term
    square_b[...] = (per_b * per_b).astype(jnp.bfloat16).reshape(square_b.shape)

    def b_copy(step):
        return pltpu.make_async_remote_copy(
            src_ref=square_b.at[lax.rem(me_d + step, GROUP)],
            dst_ref=slots_b.at[step],
            send_sem=b_send.at[step],
            recv_sem=b_recv.at[step],
            device_id=to_dp(step),
            device_id_type=MESH,
        )

    each_other(lambda step: b_copy(step).start())

    each_other(lambda step: term_copy(step).wait())
    low_slots[0] = low_terms[me_t]
    rows = LEN // GROUP
    mine = pl.ds(pl.multiple_of(me_t * rows, rows), rows)
    grad_low[mine, :] = jnp.sum(low_slots[...], axis=0).astype(jnp.bfloat16)

    def full_copy(step, owner):
        place = pl.ds(pl.multiple_of(owner * rows, rows), rows)
        return pltpu.make_async_remote_copy(
            src_ref=grad_low.at[place, :],
            dst_ref=grad_low.at[place, :],
            send_sem=full_send.at[step],
            recv_sem=full_recv.at[step],
            device_id=to_tensor(step),
            device_id_type=MESH,
        )

    each_other(lambda step: full_copy(step, me_t).start())
    each_other(lambda step: full_copy(step, me_t).wait_send())
    each_other(
        lambda step: full_copy(step, lax.rem(me_t + GROUP - step, GROUP)).wait_recv()
    )
    per_a = lax.dot_general(
        grad_low[...], attention[...], (((0,), (0,)), ((), ())), preferred_element_type=jnp.float32
    )
    square_a[...] = (per_a * per_a).astype(jnp.bfloat16).reshape(square_a.shape)

    def a_copy(step):
        return pltpu.make_async_remote_copy(
            src_ref=square_a.at[lax.rem(me_d + step, GROUP)],
            dst_ref=slots_a.at[step],
            send_sem=a_send.at[step],
            recv_sem=a_recv.at[step],
            device_id=to_dp(step),
            device_id_type=MESH,
        )

    each_other(lambda step: a_copy(step).start())

    per = ADAPTER_RANK // GROUP

    def finish(copy, squares, slots, out):
        each_other(lambda step: copy(step).wait())
        slots[0] = squares[me_d]
        total = jnp.sum(slots[...].astype(jnp.float32), axis=0)
        for adapter in range(ADAPTER_COUNT):
            chosen = None
            for step in range(PASSES):
                share = jnp.where(objective[step] == adapter, 1.0 / EXAMPLES, 0.0)
                piece = share * total[step * per : (step + 1) * per]
                chosen = piece if chosen is None else chosen + piece
            out[adapter] = chosen

    finish(b_copy, square_b, slots_b, out_b)
    finish(a_copy, square_a, slots_a, out_a)


def tail(objective, partial, low, cotangent, scale, up, attention):
    columns = partial.shape[1]
    features = attention.shape[1]
    per = ADAPTER_RANK // GROUP
    wide = PASSES * ADAPTER_RANK
    rows = LEN // GROUP
    bf16, f32 = jnp.bfloat16, jnp.float32
    vmem = pl.BlockSpec(memory_space=pltpu.VMEM)
    return pl.pallas_call(
        tail_kernel,
        name="tail",
        out_shape=(
            jax.ShapeDtypeStruct((ADAPTER_COUNT, per, features), f32),
            jax.ShapeDtypeStruct((ADAPTER_COUNT, per, columns), f32),
        ),
        in_specs=[pl.BlockSpec(memory_space=pltpu.SMEM)] + [vmem] * 6,
        out_specs=(vmem, vmem),
        scratch_shapes=[
            pltpu.VMEM((PASSES, LEN, columns), f32),
            pltpu.VMEM((PASSES, LEN, columns), bf16),
            pltpu.VMEM((PASSES, LEN, wide), bf16),
            pltpu.VMEM((PASSES, wide, columns), bf16),
            pltpu.VMEM((GROUP, 2 * PASSES, LEN), f32),
            pltpu.VMEM((GROUP, rows, wide), f32),
            pltpu.VMEM((GROUP, rows, wide), f32),
            pltpu.VMEM((LEN, wide), bf16),
            pltpu.VMEM((GROUP, wide // GROUP, columns), bf16),
            pltpu.VMEM((GROUP, wide // GROUP, columns), bf16),
            pltpu.VMEM((GROUP, wide // GROUP, features), bf16),
            pltpu.VMEM((GROUP, wide // GROUP, features), bf16),
        ]
        + [pltpu.SemaphoreType.DMA((GROUP,))] * 10,
        compiler_params=pltpu.CompilerParams(
            collective_id=0, has_side_effects=True, vmem_limit_bytes=56 * 2**20
        ),
    )(objective, partial, low, cotangent, scale, up, attention)


def body(
    attention,
    output_weight_frozen,
    residual,
    cotangent,
    output_norm_scale,
    adapter_down_weights,
    adapter_up_weights,
    objective,
):
    gathered = lax.all_gather(attention, "tensor", axis=1, tiled=True)
    low = jnp.einsum(
        "th,krh->ktr", gathered, adapter_down_weights, preferred_element_type=jnp.float32
    ).astype(jnp.bfloat16)
    base = jnp.dot(
        gathered,
        lax.all_gather(output_weight_frozen, "dp", axis=0, tiled=True),
        preferred_element_type=jnp.float32,
    )
    partial = residual.astype(jnp.float32) + base
    return tail(
        objective, partial, low, cotangent, output_norm_scale[None], adapter_up_weights, attention
    )


def solution(mesh):
    placed = (
        P("dp", "tensor"),
        P("dp", "tensor"),
        P("dp", "tensor"),
        P(None, "dp", "tensor"),
        P("tensor"),
        P(),
        P(None, None, "tensor"),
        P(),
    )
    return jax.shard_map(
        body,
        mesh=mesh,
        in_specs=placed,
        out_specs=(P(None, "dp", "tensor"), P(None, "dp", "tensor")),
        check_vma=False,
    )
```

time: 548 us -> 323 us (0.59); the launches traced: 538 us -> 323 us
  blocking collectives: 101 us -> 0 us
  waiting for transfers between devices: 347 us -> 248 us
  matrix products: 59.8 us -> 17.2 us
  Pallas kernels: 0 us -> 39.5 us
  other arithmetic: 8.09 us -> 0 us
    unnamed x4 -> x2, waiting for transfers between devices: 129 us -> 1.38 us
    psum x2 -> x0, blocking collectives: 101 us -> none  [the longest x1 66.4 us: body(): grad_low = lax.psum(low_terms, 'tensor').astype(jnp.bfloat16)]
    dot_general x28 -> x1, matrix products: 48.3 us -> 4.74 us  [body(): jnp.einsum('th,krh->ktr', gathered, adapter_down_weights, preferred_eleme...]
    pallas_call x0 -> x1, Pallas kernels: none -> 39.5 us  [tail(): pl.pallas_call(tail_kernel, name='tail', out_shape=(jax.ShapeDtypeStruct(...]
    all_gather x1, waiting for transfers between devices: 45 us -> 68 us  [body(): gathered = lax.all_gather(attention, 'tensor', axis=1, tiled=True)]
    all_gather x1, waiting for transfers between devices: 173 us -> 179 us  [body(): lax.all_gather(output_weight_frozen, 'dp', axis=0, tiled=True)]
    mul x9 -> x0, local copies, waits for them, and re-layouts: 5.95 us -> none  [the longest x4 3.05 us: body(): fisher_b = fisher_b + selector_all[step][:, None, None] * owned_b]
  transfers between devices with their start and end apart: 3 -> 2, of which waited for: 3 -> 2; matrix products, arithmetic and copies ran while one was open for 7% -> 2% of each run, Pallas kernels for 0% -> 0%
where the time goes in v1:
time: 323 us
  waiting for transfers between devices  248 us (77%)
  Pallas kernels  39.5 us (12%)
  matrix products  17.2 us (5%)
  between operations  14.1 us (4%)
  local copies, waits for them, and re-layouts  3.69 us (1%)
    all_gather x1, waiting for transfers between devices, body(): lax.all_gather(output_weight_frozen, 'dp', axis=0, tiled=True)  179 us
    all_gather x1, waiting for transfers between devices, body(): gathered = lax.all_gather(attention, 'tensor', axis=1, tiled=True)  68 us
    pallas_call x1, Pallas kernels, tail(): pl.pallas_call(tail_kernel, name='tail', out_shape=(jax.ShapeDtypeStruct(...  39.5 us
    dot_general x1, matrix products, body(): jnp.dot(gathered, lax.all_gather(output_weight_frozen, 'dp', axis=0, tile...  12.5 us
  transfers between devices with their start and end apart: 2, of which 2 were waited for; matrix products, arithmetic and copies ran while one was open for 2% of the time, Pallas kernels for 0%

profile of v1, /device:TPU:1, one launch (start us, length us, event | category | flops | bytes accessed | tf_op | source)
XLA Modules:
  0.0 322.8 jit_solution(5086068151031541413)
XLA Ops:
  7.2 0.0 all-gather.3.cloned.1.call-start
  7.2 0.7 all-gather.3.cloned.1.call-update
  7.9 0.0 all-gather.5.cloned.1.call-start
  7.9 0.7 all-gather.5.cloned.1.call-update
  8.6 0.0 copy-start
  8.7 68.0 %all-gather.3.cloned.1.call-done = bf16[256,8192]{1,0:T(8,128)(2,1)} async-done(((bf16[256,512]{1,0:T(8,128)(2,1)}), bf16[256,8192]{1,0:T(8,128)(2,1)}) %all-gather.3.cloned.1.call-update) | async-done | bytes 4194320 | tf_op jit(solution)/shard_map/all_gather | solution.py:285
  76.6 4.7 %fusion.2 = bf16[4,64,256]{2,1,0:T(8,128)(2,1)S(1)} fusion(bf16[4,64,8192]{2,1,0:T(8,128)(2,1)} %param.13, bf16[256,8192]{1,0:T(8,128)(2,1)} %all-gather.3.cloned.1.call-done), kind=kOutput, calls=%fused_computation.3 | convolution fusion | flops 1073807360 | bytes 8519680 | tf_op jit(solution)/shard_map/th,krh->ktr/dot_general | solution.py:286
  81.4 0.8 copy.11
  82.2 178.9 %all-gather.5.cloned.1.call-done = bf16[8192,1024]{1,0:T(8,128)(2,1)} async-done(((bf16[512,1024]{1,0:T(8,128)(2,1)}), bf16[8192,1024]{1,0:T(8,128)(2,1)}) %all-gather.5.cloned.1.call-update) | async-done | bytes 16777232 | tf_op jit(solution)/shard_map/all_gather | solution.py:291
  261.1 0.0 copy-done
  261.1 12.5 %convolution_add_fusion.partial = f32[256,1024]{1,0:T(8,128)} fusion(bf16[256,8192]{1,0:T(8,128)(2,1)} %all-gather.3.cloned.1.call-done, bf16[8192,1024]{1,0:T(8,128)(2,1)} %all-gather.5.cloned.1.call-done, bf16[256,1024]{1,0:T(8,128)(2,1)S(1)} %copy-done), kind=kOutput, calls=%fused_computation.2 | convolution fusion | flops 4295491584 | bytes 22544384 | tf_op jit(solution)/shard_map/dot_general | solution.py:289
  273.6 39.5 %tail.1 = (f32[4,4,512]{2,1,0:T(4,128)}, f32[4,4,1024]{2,1,0:T(4,128)}) custom-call(s32[4]{0:T(128)} %objective.1, f32[256,1024]{1,0:T(8,128)} %convolution_add_fusion.partial, bf16[4,256,64]{2,1,0:T(8,128)(2,1)} %bitcast.10, bf16[4,256,1024]{2,1,0:T(8,128)(2,1)} %cotangent.1, f32[1,1024]{1,0:T(1,128)} %bitcast.11, bf16[4,64,1024]{2,1,0:T(8,128)(2,1)} %up.1, ...), custom_call_target="tpu_custom_call" | custom-call | tf_op jit(solution)/shard_map/tail/pallas_call | solution.py:245
  313.1 1.4 copy.14
  314.5 1.5 copy.15
Async XLA Ops:
  7.2 69.5 %all-gather.3.cloned.1.call-start = ((), (), s32[]{:S(2)}) async-start(), calls=%async_computation | async-start | bytes 4456448 | tf_op jit(solution)/shard_map/all_gather | solution.py:285
  7.9 253.2 %all-gather.5.cloned.1.call-start = ((), (), s32[]{:S(2)}) async-start(), calls=%async_computation.1 | async-start | bytes 17825792 | tf_op jit(solution)/shard_map/all_gather | solution.py:291
  8.6 252.4 %copy-start = (bf16[256,1024]{1,0:T(8,128)(2,1)S(1)}, bf16[256,1024]{1,0:T(8,128)(2,1)}, u32[]{:S(2)}) copy-start(bf16[256,1024]{1,0:T(8,128)(2,1)} %param.10) | copy-start | bytes 1572868
Sparse Core Ops, SparseCore 0:
  10.6 65.9 all-gather.2
  78.4 182.6 all-gather.4

commit v2 on v0

v2 whole, which is shorter than its diff:
```python
import jax
import jax.numpy as jnp
from jax import lax
from jax.experimental import pallas as pl
from jax.experimental.pallas import tpu as pltpu
from jax.sharding import PartitionSpec as P

MODEL_WIDTH = 16384
ADAPTER_RANK = 64
ADAPTER_COUNT = 4
PASSES = 4
LEN = 256
EXAMPLES = 16
GROUP = 16
MESH = pl.DeviceIdType.MESH

epsilon = 1e-05


def to_tensor(step):
    return (lax.axis_index("dp"), lax.rem(lax.axis_index("tensor") + step, GROUP))


def to_dp(step):
    return (lax.rem(lax.axis_index("dp") + step, GROUP), lax.axis_index("tensor"))


def each_other(action):
    def one(step, carry):
        action(step)
        return carry

    lax.fori_loop(1, GROUP, one, 0)


RING = 8
NEAR = (4, 3, -3, 2, -2, 1, -1, 0)
CHUNK = 256
PIECE = 32


def spread(picked, step):
    per = ADAPTER_RANK // GROUP
    size = (ADAPTER_COUNT * ADAPTER_RANK, PASSES * ADAPTER_RANK)
    row = lax.broadcasted_iota(jnp.int32, size, 0)
    col = lax.broadcasted_iota(jnp.int32, size, 1)
    goal = picked * ADAPTER_RANK + col // (PASSES * per) * per + col % per
    chosen = (row == goal) & (col // per % PASSES == step)
    return jnp.where(chosen, 1.0, 0.0).astype(jnp.bfloat16)


def remote(src, dst, send, recv, device):
    return pltpu.make_async_remote_copy(
        src_ref=src,
        dst_ref=dst,
        send_sem=send,
        recv_sem=recv,
        device_id=device,
        device_id_type=MESH,
    )


def whole_kernel(
    objective,
    scale,
    attention,
    weight_hbm,
    residual_hbm,
    cotangent_hbm,
    down_hbm,
    up_hbm,
    out_a,
    out_b,
    tokens,
    weight,
    residual,
    cotangent,
    down,
    up,
    ring_out,
    ring_in,
    hidden,
    sums,
    grads,
    low_terms,
    low_slots,
    low_all,
    low_wide,
    up_wide,
    stat_slots,
    back_terms,
    back_slots,
    back_all,
    square_b,
    slots_b,
    square_a,
    slots_a,
    local,
    first_send,
    first_recv,
    weight_send,
    weight_recv,
    y_send,
    y_recv,
    f_send,
    f_recv,
    core_send,
    core_recv,
    ring_send,
    ring_recv,
    low_sems,
    back_sems,
    stat_send,
    stat_recv,
    b_send,
    b_recv,
    a_send,
    a_recv,
):
    me_d = lax.axis_index("dp")
    me_t = lax.axis_index("tensor")
    half = me_d // RING
    me_z = lax.rem(me_d, RING)
    side = me_t // RING
    goal_z = lax.rem(me_t, RING)
    me_y = me_t // 4
    core = lax.rem(me_t, 2)
    has_own = goal_z == me_z
    rows = LEN // GROUP
    wide = PASSES * ADAPTER_RANK
    columns = weight.shape[2]
    chunks = columns // CHUNK
    features = attention.shape[1]

    barrier = pltpu.get_barrier_semaphore()

    def greet(step):
        pl.semaphore_signal(barrier, inc=1, device_id=to_tensor(step), device_id_type=MESH)
        pl.semaphore_signal(barrier, inc=1, device_id=to_dp(step), device_id_type=MESH)

    each_other(greet)

    def greet_sender(number, carry):
        z = number // 2
        t = lax.rem(number, 2) * RING + me_z

        @pl.when((z != me_z) | (t != me_t))
        def _():
            pl.semaphore_signal(
                barrier, inc=1, device_id=(half * RING + z, t), device_id_type=MESH
            )

        return carry

    lax.fori_loop(0, 2 * RING, greet_sender, 0)

    def load(number):
        place = pl.ds(pl.multiple_of(me_t * features, features), features)
        pairs = (
            (down_hbm.at[:, :, place], down),
            (weight_hbm, weight.at[half]),
            (up_hbm, up),
            (residual_hbm, residual),
            (cotangent_hbm, cotangent),
        )
        return pltpu.make_async_copy(*pairs[number], local.at[number])

    for number in range(5):
        load(number).start()

    load(0).wait()
    low_terms[...] = lax.dot_general(
        attention[...],
        down[...].reshape(ADAPTER_COUNT * ADAPTER_RANK, features),
        (((1,), (1,)), ((), ())),
        preferred_element_type=jnp.float32,
    ).reshape(low_terms.shape)

    pl.semaphore_wait(barrier, 2 * (GROUP - 1) + 2 * RING - jnp.where(has_own, 1, 0))

    def piece(t):
        number = t // 4 * 2 + lax.rem(t, 2)
        return pl.ds(pl.multiple_of(number * PIECE, PIECE), PIECE)

    def first_copy(step):
        t = lax.rem(me_t + step, GROUP)
        return remote(
            attention.at[piece(t), :],
            tokens.at[me_z, side, piece(t), :],
            first_send.at[step],
            first_recv.at[me_z * 2 + side],
            (half * RING + goal_z, t),
        )

    each_other(lambda step: first_copy(step).start())

    @pl.when(has_own)
    def _():
        tokens[me_z, side, piece(me_t), :] = attention[piece(me_t), :]

    @pl.when(jnp.logical_not(has_own))
    def _():
        first_copy(0).start()

    def weight_copy(chunk, slot):
        place = pl.ds(chunk * CHUNK, CHUNK)
        return remote(
            weight_hbm.at[:, place],
            weight.at[slot, :, place],
            weight_send.at[chunk],
            weight_recv.at[chunk],
            (lax.rem(me_d + RING, GROUP), me_t),
        )

    for chunk in range(chunks):
        weight_copy(chunk, half).start()

    def add_rows(terms, slots, total, sems):
        def term_copy(step):
            return remote(
                terms.at[lax.rem(me_t + step, GROUP)],
                slots.at[step],
                sems.at[0, step],
                sems.at[1, step],
                to_tensor(step),
            )

        def full_copy(step, owner):
            place = pl.ds(pl.multiple_of(owner * rows, rows), rows)
            return remote(
                total.at[place, :],
                total.at[place, :],
                sems.at[2, step],
                sems.at[3, step],
                to_tensor(step),
            )

        def begin():
            each_other(lambda step: term_copy(step).start())

        def middle():
            each_other(lambda step: term_copy(step).wait())
            slots[0] = terms[me_t]
            mine = pl.ds(pl.multiple_of(me_t * rows, rows), rows)
            total[mine, :] = jnp.sum(slots[...], axis=0).astype(jnp.bfloat16)
            each_other(lambda step: full_copy(step, me_t).start())

        def end():
            each_other(lambda step: full_copy(step, me_t).wait_send())
            each_other(
                lambda step: full_copy(step, lax.rem(me_t + GROUP - step, GROUP)).wait_recv()
            )

        return begin, middle, end

    low_begin, low_middle, low_end = add_rows(low_terms, low_slots, low_all, low_sems)
    back_begin, back_middle, back_end = add_rows(back_terms, back_slots, back_all, back_sems)
    low_begin()

    def at_y(shift):
        return lax.rem(me_t + (shift % 4) * 4, GROUP)

    other = me_t + 1 - 2 * core

    def z_of(number):
        return lax.rem(me_z + NEAR[number] + RING, RING)

    def y_copy(number, way, owner):
        part = tokens.at[z_of(number), :, piece(owner), :]
        return remote(
            part, part, y_send.at[number, way], y_recv.at[number, way], (me_d, at_y((1, -1)[way]))
        )

    def f_copy(number, way, owner):
        part = tokens.at[z_of(number), way, piece(owner), :]
        return remote(
            part, part, f_send.at[number, way], f_recv.at[number, way], (me_d, at_y((1, -1)[way]))
        )

    def core_copy(number, shift, owner):
        part = tokens.at[z_of(number), :, piece(owner), :]
        return remote(
            part, part, core_send.at[number, shift], core_recv.at[number, shift], (me_d, other)
        )

    def spread_own(number):
        z = z_of(number)
        for h in range(2):
            wait = remote(
                attention.at[piece(me_t), :],
                tokens.at[z, h, piece(me_t), :],
                first_send.at[0],
                first_recv.at[z * 2 + h],
                (me_d, other),
            ).wait_recv
            if NEAR[number] == 0:
                pl.when(jnp.logical_not(has_own & (side == h)))(wait)
            else:
                wait()
        y_copy(number, 0, me_t).start()
        y_copy(number, 1, me_t).start()
        core_copy(number, 0, me_t).start()

    def spread_next(number):
        y_copy(number, 0, at_y(-1)).wait_recv()
        f_copy(number, 0, at_y(-1)).start()
        core_copy(number, 3, at_y(-1)).start()
        y_copy(number, 1, at_y(1)).wait_recv()
        f_copy(number, 1, at_y(1)).start()
        core_copy(number, 1, at_y(1)).start()

    def spread_last(number):
        f_copy(number, 0, at_y(2)).wait_recv()
        f_copy(number, 1, at_y(2)).wait_recv()
        core_copy(number, 2, at_y(2)).start()

    def arrived(number):
        for shift in range(4):
            owner = lax.rem(other + shift * 4, GROUP)
            core_copy(number, shift, owner).wait_recv()

    def product(number, cols):
        z = z_of(number)
        total = jnp.dot(tokens[z, 0], weight[0, :, cols], preferred_element_type=jnp.float32)
        return total + jnp.dot(
            tokens[z, 1], weight[1, :, cols], preferred_element_type=jnp.float32
        )

    def ring_copy(way, far, chunk, slot):
        if far == 4:
            place = pl.ds(way * (LEN // 2), LEN // 2)
        else:
            place = pl.ds(0, LEN)
        z = lax.rem(me_z + (1, RING - 1)[way], RING)
        return remote(
            ring_out.at[way, far - 1, chunk, place, :],
            ring_in.at[way, far - 1, chunk, place, :],
            ring_send.at[way, far - 1, chunk],
            ring_recv.at[way, far - 1, chunk],
            (half * RING + z, me_t),
        )

    def cols_of(chunk):
        return pl.ds(pl.multiple_of(chunk * CHUNK, CHUNK), CHUNK)

    def send_products(far, begin):
        def one(chunk, carry):
            cols = cols_of(chunk)
            if far == 4:
                value = product(0, cols).astype(jnp.bfloat16)
                for way in range(2):
                    mine = slice(way * (LEN // 2), (way + 1) * (LEN // 2))
                    ring_out[way, 3, chunk, mine, :] = value[mine]
                    ring_copy(way, 4, chunk, 0).start()
                return carry
            for way in range(2):
                number = NEAR.index((far, -far)[way])
                value = product(number, cols)
                ring_copy(way, far + 1, chunk, 0).wait_recv()
                if far == 3:
                    mine = slice(way * (LEN // 2), (way + 1) * (LEN // 2))
                    rest = slice((1 - way) * (LEN // 2), (2 - way) * (LEN // 2))
                    ring_out[way, 2, chunk, mine, :] = (
                        value[mine] + ring_in[way, 3, chunk, mine, :].astype(jnp.float32)
                    ).astype(jnp.bfloat16)
                    ring_out[way, 2, chunk, rest, :] = value[rest].astype(jnp.bfloat16)
                else:
                    ring_out[way, far - 1, chunk] = (
                        value + ring_in[way, far, chunk].astype(jnp.float32)
                    ).astype(jnp.bfloat16)
                ring_copy(way, far, chunk, 0).start()
            return carry

        lax.fori_loop(begin, begin + chunks // 2, one, 0)

    def own_products(begin):
        def one(chunk, carry):
            cols = cols_of(chunk)
            value = product(NEAR.index(0), cols)
            for way in range(2):
                ring_copy(way, 1, chunk, 0).wait_recv()
                value = value + ring_in[way, 0, chunk].astype(jnp.float32)
            value = value + residual[:, cols].astype(jnp.float32)
            for step in range(PASSES):
                here = value + jnp.dot(
                    low_wide[step], up_wide[step, :, cols], preferred_element_type=jnp.float32
                )
                hidden[step, :, cols] = here
                weighted = cotangent[step, :, cols].astype(jnp.float32) * scale[:, cols]
                squares = here * here
                inner = weighted * here
                sums[2 * step] += squares[:, :128] + squares[:, 128:]
                sums[2 * step + 1] += inner[:, :128] + inner[:, 128:]
            return carry

        lax.fori_loop(begin, begin + chunks // 2, one, 0)

    spread_own(0)
    spread_own(1)
    spread_own(2)
    spread_next(0)
    spread_own(3)
    spread_next(1)
    spread_last(0)
    spread_own(4)
    spread_next(2)
    spread_last(1)
    load(1).wait()
    for chunk in range(chunks // 2):
        weight_copy(chunk, 1 - half).wait_recv()
    arrived(0)
    send_products(4, 0)
    spread_own(5)
    spread_next(3)
    spread_last(2)
    arrived(1)
    arrived(2)
    send_products(3, 0)
    spread_own(6)
    spread_next(4)
    spread_last(3)
    spread_own(7)
    spread_next(5)
    spread_last(4)
    arrived(3)
    arrived(4)
    send_products(2, 0)
    spread_next(6)
    spread_last(5)
    spread_next(7)
    spread_last(6)
    arrived(5)
    arrived(6)
    send_products(1, 0)
    spread_last(7)
    arrived(7)
    for chunk in range(chunks // 2, chunks):
        weight_copy(chunk, 1 - half).wait_recv()
    send_products(4, chunks // 2)
    low_middle()
    send_products(3, chunks // 2)
    low_end()
    for number in range(2, 5):
        load(number).wait()
    up_rows = up[...].reshape(ADAPTER_COUNT * ADAPTER_RANK, columns)
    for step in range(PASSES):
        choice = spread(objective[step], step)
        low_wide[step] = jnp.dot(
            low_all[...], choice, preferred_element_type=jnp.float32
        ).astype(jnp.bfloat16)
        up_wide[step] = lax.dot_general(
            choice, up_rows, (((0,), (0,)), ((), ())), preferred_element_type=jnp.float32
        ).astype(jnp.bfloat16)
    sums[...] = jnp.zeros(sums.shape, jnp.float32)
    send_products(2, chunks // 2)
    own_products(0)
    send_products(1, chunks // 2)
    own_products(chunks // 2)

    lane = lax.broadcasted_iota(jnp.int32, (LEN, 128), 1)
    stats = jnp.zeros((LEN, 128), jnp.float32)
    for kind in range(2 * PASSES):
        stats = jnp.where(lane == kind, jnp.sum(sums[kind], axis=1, keepdims=True), stats)
    stat_slots[0] = stats.T[: 2 * PASSES]

    def stat_copy(step):
        return remote(
            stat_slots.at[0],
            stat_slots.at[step],
            stat_send.at[step],
            stat_recv.at[step],
            to_tensor(step),
        )

    each_other(lambda step: stat_copy(step).start())
    each_other(lambda step: stat_copy(step).wait())
    totals = jnp.sum(stat_slots[...], axis=0)
    inner_first = jnp.concatenate([totals[1:], totals[:1]], axis=0)
    scale_inv = lax.rsqrt(totals / MODEL_WIDTH + epsilon)
    weight_hidden = inner_first * scale_inv**3 / MODEL_WIDTH
    keep = jnp.concatenate(
        [scale_inv, weight_hidden, jnp.zeros((128 - 4 * PASSES, LEN), jnp.float32)], axis=0
    )
    keep = jnp.where(lax.broadcasted_iota(jnp.int32, keep.shape, 0) % 2 == 0, keep, 0.0)
    by_token = keep.T

    terms = None
    for step in range(PASSES):
        weighted = cotangent[step].astype(jnp.float32) * scale[...]
        per_token = by_token[:, 2 * step : 2 * step + 1]
        back = by_token[:, 2 * PASSES + 2 * step : 2 * PASSES + 2 * step + 1]
        grads[step] = (per_token * weighted - hidden[step] * back).astype(jnp.bfloat16)
        term = lax.dot_general(
            grads[step], up_wide[step], (((1,), (1,)), ((), ())), preferred_element_type=jnp.float32
        )
        terms = term if terms is None else terms + term
    back_terms[...] = terms.reshape(back_terms.shape)
    back_begin()

    per_b = None
    for step in range(PASSES):
        term = lax.dot_general(
            low_wide[step], grads[step], (((0,), (0,)), ((), ())), preferred_element_type=jnp.float32
        )
        per_b = term if per_b is None else per_b + term
    square_b[...] = (per_b * per_b).astype(jnp.bfloat16).reshape(square_b.shape)

    def owner_copy(step, squares, slots, send, recv):
        return remote(
            squares.at[lax.rem(me_d + step, GROUP)],
            slots.at[step],
            send.at[step],
            recv.at[step],
            to_dp(step),
        )

    each_other(lambda step: owner_copy(step, square_b, slots_b, b_send, b_recv).start())

    back_middle()
    back_end()
    per_a = lax.dot_general(
        back_all[...], attention[...], (((0,), (0,)), ((), ())), preferred_element_type=jnp.float32
    )
    square_a[...] = (per_a * per_a).astype(jnp.bfloat16).reshape(square_a.shape)
    each_other(lambda step: owner_copy(step, square_a, slots_a, a_send, a_recv).start())

    per = ADAPTER_RANK // GROUP

    def finish(squares, slots, send, recv, out):
        each_other(lambda step: owner_copy(step, squares, slots, send, recv).wait())
        slots[0] = squares[me_d]
        total = jnp.sum(slots[...].astype(jnp.float32), axis=0)
        for adapter in range(ADAPTER_COUNT):
            chosen = None
            for step in range(PASSES):
                share = jnp.where(objective[step] == adapter, 1.0 / EXAMPLES, 0.0)
                part = share * total[step * per : (step + 1) * per]
                chosen = part if chosen is None else chosen + part
            out[adapter] = chosen

    finish(square_b, slots_b, b_send, b_recv, out_b)

    each_other(lambda step: first_copy(step).wait_send())
    pl.when(jnp.logical_not(has_own))(lambda: first_copy(0).wait_send())
    for chunk in range(chunks):
        weight_copy(chunk, half).wait_send()
    for number in range(RING):
        for way in range(2):
            y_copy(number, way, me_t).wait_send()
            f_copy(number, way, me_t).wait_send()
        for shift in range(4):
            core_copy(number, shift, me_t).wait_send()

    def ring_done(chunk, carry):
        for way in range(2):
            for far in range(1, 5):
                ring_copy(way, far, chunk, 0).wait_send()
        return carry

    lax.fori_loop(0, chunks, ring_done, 0)
    finish(square_a, slots_a, a_send, a_recv, out_a)


def body(
    attention,
    output_weight_frozen,
    residual,
    cotangent,
    output_norm_scale,
    adapter_down_weights,
    adapter_up_weights,
    objective,
):
    features = attention.shape[1]
    depth, columns = output_weight_frozen.shape
    chunks = columns // CHUNK
    per = ADAPTER_RANK // GROUP
    wide = PASSES * ADAPTER_RANK
    rows = LEN // GROUP
    bf16, f32 = jnp.bfloat16, jnp.float32
    vmem = pl.BlockSpec(memory_space=pltpu.VMEM)
    hbm = pl.BlockSpec(memory_space=pl.ANY)
    sem = pltpu.SemaphoreType.DMA
    return pl.pallas_call(
        whole_kernel,
        name="fisher",
        out_shape=(
            jax.ShapeDtypeStruct((ADAPTER_COUNT, per, features), f32),
            jax.ShapeDtypeStruct((ADAPTER_COUNT, per, columns), f32),
        ),
        in_specs=[pl.BlockSpec(memory_space=pltpu.SMEM), vmem, vmem] + [hbm] * 5,
        out_specs=(vmem, vmem),
        scratch_shapes=[
            pltpu.VMEM((RING, 2, LEN, features), bf16),
            pltpu.VMEM((2, depth, columns), bf16),
            pltpu.VMEM((LEN, columns), bf16),
            pltpu.VMEM((PASSES, LEN, columns), bf16),
            pltpu.VMEM((ADAPTER_COUNT, ADAPTER_RANK, features), bf16),
            pltpu.VMEM((ADAPTER_COUNT, ADAPTER_RANK, columns), bf16),
            pltpu.VMEM((2, 4, chunks, LEN, CHUNK), bf16),
            pltpu.VMEM((2, 4, chunks, LEN, CHUNK), bf16),
            pltpu.VMEM((PASSES, LEN, columns), f32),
            pltpu.VMEM((2 * PASSES, LEN, 128), f32),
            pltpu.VMEM((PASSES, LEN, columns), bf16),
            pltpu.VMEM((GROUP, rows, wide), f32),
            pltpu.VMEM((GROUP, rows, wide), f32),
            pltpu.VMEM((LEN, wide), bf16),
            pltpu.VMEM((PASSES, LEN, wide), bf16),
            pltpu.VMEM((PASSES, wide, columns), bf16),
            pltpu.VMEM((GROUP, 2 * PASSES, LEN), f32),
            pltpu.VMEM((GROUP, rows, wide), f32),
            pltpu.VMEM((GROUP, rows, wide), f32),
            pltpu.VMEM((LEN, wide), bf16),
            pltpu.VMEM((GROUP, wide // GROUP, columns), bf16),
            pltpu.VMEM((GROUP, wide // GROUP, columns), bf16),
            pltpu.VMEM((GROUP, wide // GROUP, features), bf16),
            pltpu.VMEM((GROUP, wide // GROUP, features), bf16),
            sem((5,)),
            sem((GROUP,)),
            sem((GROUP,)),
            sem((chunks,)),
            sem((chunks,)),
            sem((RING, 2)),
            sem((RING, 2)),
            sem((RING, 2)),
            sem((RING, 2)),
            sem((RING, 4)),
            sem((RING, 4)),
            sem((2, 4, chunks)),
            sem((2, 4, chunks)),
            sem((4, GROUP)),
            sem((4, GROUP)),
        ]
        + [sem((GROUP,))] * 6,
        compiler_params=pltpu.CompilerParams(
            collective_id=0, has_side_effects=True, vmem_limit_bytes=56 * 2**20
        ),
    )(
        objective,
        output_norm_scale[None],
        attention,
        output_weight_frozen,
        residual,
        cotangent,
        adapter_down_weights,
        adapter_up_weights,
    )


def solution(mesh):
    placed = (
        P("dp", "tensor"),
        P("dp", "tensor"),
        P("dp", "tensor"),
        P(None, "dp", "tensor"),
        P("tensor"),
        P(),
        P(None, None, "tensor"),
        P(),
    )
    return jax.shard_map(
        body,
        mesh=mesh,
        in_specs=placed,
        out_specs=(P(None, "dp", "tensor"), P(None, "dp", "tensor")),
        check_vma=False,
    )
```

time: 548 us -> 138 us (0.25); the launches traced: 538 us -> 138 us
  waiting for transfers between devices: 347 us -> 0 us
  Pallas kernels: 0 us -> 135 us
  blocking collectives: 101 us -> 0 us
  matrix products: 59.8 us -> 0 us
  between operations: 14.7 us -> 0.64 us
  other arithmetic: 8.09 us -> 0 us
    all_gather x2 -> x0, waiting for transfers between devices: 218 us -> none  [the longest x1 173 us: body(): lax.all_gather(output_weight_frozen, 'dp', axis=0, tiled=True)]
    pallas_call x0 -> x1, Pallas kernels: none -> 135 us  [body(): pl.pallas_call(whole_kernel, name='fisher', out_shape=(jax.ShapeDtypeStru...]
    unnamed x4 -> x0, waiting for transfers between devices: 129 us -> none
    psum x2 -> x0, blocking collectives: 101 us -> none  [the longest x1 66.4 us: body(): grad_low = lax.psum(low_terms, 'tensor').astype(jnp.bfloat16)]
    dot_general x29 -> x0, matrix products: 59.8 us -> none  [the longest x4 19.3 us: body(): jnp.einsum('tf,fqb->tqb', adapter_picker, adapter_down_weights, preferred...]
    mul x9 -> x0, local copies, waits for them, and re-layouts: 5.95 us -> none  [the longest x4 3.05 us: body(): fisher_b = fisher_b + selector_all[step][:, None, None] * owned_b]
  transfers between devices with their start and end apart: 3 -> 0, of which waited for: 3 -> 0; matrix products, arithmetic and copies ran while one was open for 7% -> 0% of each run, Pallas kernels for 0% -> 0%
where the time goes in v2:
time: 138 us
  Pallas kernels  135 us (98%)
  local copies, waits for them, and re-layouts  2.85 us (2%)
    pallas_call x1, Pallas kernels, body(): pl.pallas_call(whole_kernel, name='fisher', out_shape=(jax.ShapeDtypeStru...  135 us
    unnamed x2, local copies, waits for them, and re-layouts  2.85 us

profile of v2, /device:TPU:1, one launch (start us, length us, event | category | flops | bytes accessed | tf_op | source)
XLA Modules:
  0.0 138.1 jit_solution(18109351926945439573)
XLA Ops:
  0.6 134.6 %fisher.1 = (f32[4,4,512]{2,1,0:T(4,128)}, f32[4,4,1024]{2,1,0:T(4,128)}) custom-call(s32[4]{0:T(128)} %objective.1, f32[1,1024]{1,0:T(1,128)} %bitcast.1, bf16[256,512]{1,0:T(8,128)(2,1)} %attention.1, bf16[512,1024]{1,0:T(8,128)(2,1)} %weight_hbm.1, bf16[256,1024]{1,0:T(8,128)(2,1)} %residual_hbm.1, bf16[4,256,1024]{2,1,0:T(8,128)(2,1)} %cotangent_hbm.1, ...), custom_call_target="tpu_custom_call" | custom-call | tf_op jit(solution)/shard_map/fisher/pallas_call | solution.py:584
  135.3 1.4 copy.12
  136.6 1.5 %copy.13 = f32[4,4,1024]{2,1,0:T(4,128)} copy(f32[4,4,1024]{2,1,0:T(4,128)} %get-tuple-element.5) | data formatting | bytes 131072

commit v3 on v2

--- a/solution.py
+++ b/solution.py
@@ -71,6 +71,7 @@
     up_hbm,
     out_a,
     out_b,
+    middle,
     tokens,
     weight,
     residual,
@@ -96,8 +97,10 @@
     square_a,
     slots_a,
     local,
-    first_send,
-    first_recv,
+    plane_send,
+    plane_recv,
+    z_send,
+    z_recv,
     weight_send,
     weight_recv,
     y_send,
@@ -121,11 +124,7 @@
     me_t = lax.axis_index("tensor")
     half = me_d // RING
     me_z = lax.rem(me_d, RING)
-    side = me_t // RING
-    goal_z = lax.rem(me_t, RING)
-    me_y = me_t // 4
     core = lax.rem(me_t, 2)
-    has_own = goal_z == me_z
     rows = LEN // GROUP
     wide = PASSES * ADAPTER_RANK
     columns = weight.shape[2]
@@ -139,20 +138,6 @@
         pl.semaphore_signal(barrier, inc=1, device_id=to_dp(step), device_id_type=MESH)
 
     each_other(greet)
-
-    def greet_sender(number, carry):
-        z = number // 2
-        t = lax.rem(number, 2) * RING + me_z
-
-        @pl.when((z != me_z) | (t != me_t))
-        def _():
-            pl.semaphore_signal(
-                barrier, inc=1, device_id=(half * RING + z, t), device_id_type=MESH
-            )
-
-        return carry
-
-    lax.fori_loop(0, 2 * RING, greet_sender, 0)
 
     def load(number):
         place = pl.ds(pl.multiple_of(me_t * features, features), features)
@@ -176,31 +161,24 @@
         preferred_element_type=jnp.float32,
     ).reshape(low_terms.shape)
 
-    pl.semaphore_wait(barrier, 2 * (GROUP - 1) + 2 * RING - jnp.where(has_own, 1, 0))
+    pl.semaphore_wait(barrier, 2 * (GROUP - 1))
 
     def piece(t):
         number = t // 4 * 2 + lax.rem(t, 2)
         return pl.ds(pl.multiple_of(number * PIECE, PIECE), PIECE)
 
-    def first_copy(step):
+    def plane_copy(step, source):
         t = lax.rem(me_t + step, GROUP)
         return remote(
             attention.at[piece(t), :],
-            tokens.at[me_z, side, piece(t), :],
-            first_send.at[step],
-            first_recv.at[me_z * 2 + side],
-            (half * RING + goal_z, t),
-        )
-
-    each_other(lambda step: first_copy(step).start())
-
-    @pl.when(has_own)
-    def _():
-        tokens[me_z, side, piece(me_t), :] = attention[piece(me_t), :]
-
-    @pl.when(jnp.logical_not(has_own))
-    def _():
-        first_copy(0).start()
+            middle.at[lax.rem(source, RING), source // RING],
+            plane_send.at[step],
+            plane_recv.at[source],
+            (me_d, t),
+        )
+
+    each_other(lambda step: plane_copy(step, me_t).start())
+    middle[lax.rem(me_t, RING), me_t // RING] = attention[piece(me_t), :]
 
     def weight_copy(chunk, slot):
         place = pl.ds(chunk * CHUNK, CHUNK)
@@ -283,20 +261,29 @@
             part, part, core_send.at[number, shift], core_recv.at[number, shift], (me_d, other)
         )
 
+    def z_copy(number, source):
+        goal = z_of(number)
+        return remote(
+            middle.at[goal],
+            tokens.at[source, :, piece(me_t), :],
+            z_send.at[number],
+            z_recv.at[source],
+            (half * RING + goal, me_t),
+        )
+
+    def along_z(number):
+        goal = z_of(number)
+        for h in range(2):
+            source = goal + h * RING
+            pl.when(source != me_t)(plane_copy(1, source).wait_recv)
+        if NEAR[number] == 0:
+            tokens[me_z, :, piece(me_t), :] = middle[me_z]
+        else:
+            z_copy(number, me_z).start()
+
     def spread_own(number):
-        z = z_of(number)
-        for h in range(2):
-            wait = remote(
-                attention.at[piece(me_t), :],
-                tokens.at[z, h, piece(me_t), :],
-                first_send.at[0],
-                first_recv.at[z * 2 + h],
-                (me_d, other),
-            ).wait_recv
-            if NEAR[number] == 0:
-                pl.when(jnp.logical_not(has_own & (side == h)))(wait)
-            else:
-                wait()
+        if NEAR[number] != 0:
+            z_copy(number, z_of(number)).wait_recv()
         y_copy(number, 0, me_t).start()
         y_copy(number, 1, me_t).start()
         core_copy(number, 0, me_t).start()
@@ -395,6 +382,8 @@
 
         lax.fori_loop(begin, begin + chunks // 2, one, 0)
 
+    for number in range(RING):
+        along_z(number)
     spread_own(0)
     spread_own(1)
     spread_own(2)
@@ -540,8 +529,9 @@
 
     finish(square_b, slots_b, b_send, b_recv, out_b)
 
-    each_other(lambda step: first_copy(step).wait_send())
-    pl.when(jnp.logical_not(has_own))(lambda: first_copy(0).wait_send())
+    each_other(lambda step: plane_copy(step, me_t).wait_send())
+    for number in range(RING - 1):
+        z_copy(number, me_z).wait_send()
     for chunk in range(chunks):
         weight_copy(chunk, half).wait_send()
     for number in range(RING):
@@ -591,6 +581,7 @@
         in_specs=[pl.BlockSpec(memory_space=pltpu.SMEM), vmem, vmem] + [hbm] * 5,
         out_specs=(vmem, vmem),
         scratch_shapes=[
+            pltpu.VMEM((RING, 2, PIECE, features), bf16),
             pltpu.VMEM((RING, 2, LEN, features), bf16),
             pltpu.VMEM((2, depth, columns), bf16),
             pltpu.VMEM((LEN, columns), bf16),
@@ -618,6 +609,8 @@
             sem((5,)),
             sem((GROUP,)),
             sem((GROUP,)),
+            sem((RING,)),
+            sem((RING,)),
             sem((chunks,)),
             sem((chunks,)),
             sem((RING, 2)),

time: 138 us -> 124 us (0.90)
  Pallas kernels: 135 us -> 120 us
    pallas_call x1, Pallas kernels: 135 us -> 120 us  [body(): pl.pallas_call(whole_kernel, name='fisher', out_shape=(jax.ShapeDtypeStru...]
where the time goes in v3:
time: 124 us; the launch traced here: 123 us
  Pallas kernels  120 us (97%)
  local copies, waits for them, and re-layouts  2.85 us (2%)
    pallas_call x1, Pallas kernels, body(): pl.pallas_call(whole_kernel, name='fisher', out_shape=(jax.ShapeDtypeStru...  120 us
    unnamed x2, local copies, waits for them, and re-layouts  2.85 us

profile of v3, /device:TPU:1, one launch (start us, length us, event | category | flops | bytes accessed | tf_op | source)
XLA Modules:
  0.0 123.5 jit_solution(5860732684926696231)
XLA Ops:
  0.6 120.0 %fisher.1 = (f32[4,4,512]{2,1,0:T(4,128)}, f32[4,4,1024]{2,1,0:T(4,128)}) custom-call(s32[4]{0:T(128)} %objective.1, f32[1,1024]{1,0:T(1,128)} %bitcast.1, bf16[256,512]{1,0:T(8,128)(2,1)} %attention.1, bf16[512,1024]{1,0:T(8,128)(2,1)} %weight_hbm.1, bf16[256,1024]{1,0:T(8,128)(2,1)} %residual_hbm.1, bf16[4,256,1024]{2,1,0:T(8,128)(2,1)} %cotangent_hbm.1, ...), custom_call_target="tpu_custom_call" | custom-call | tf_op jit(solution)/shard_map/fisher/pallas_call | solution.py:574
  120.6 1.4 %copy.12 = f32[4,4,512]{2,1,0:T(4,128)} copy(f32[4,4,512]{2,1,0:T(4,128)} %get-tuple-element.4) | data formatting | bytes 65536
  122.0 1.5 %copy.13 = f32[4,4,1024]{2,1,0:T(4,128)} copy(f32[4,4,1024]{2,1,0:T(4,128)} %get-tuple-element.5) | data formatting | bytes 131072

commit v4 on v3

--- a/solution.py
+++ b/solution.py
@@ -37,6 +37,7 @@
 NEAR = (4, 3, -3, 2, -2, 1, -1, 0)
 CHUNK = 256
 PIECE = 32
+DIRECT = 3
 
 
 def spread(picked, step):
@@ -101,6 +102,8 @@
     plane_recv,
     z_send,
     z_recv,
+    x_send,
+    x_recv,
     weight_send,
     weight_recv,
     y_send,
@@ -153,32 +156,32 @@
     for number in range(5):
         load(number).start()
 
-    load(0).wait()
-    low_terms[...] = lax.dot_general(
-        attention[...],
-        down[...].reshape(ADAPTER_COUNT * ADAPTER_RANK, features),
-        (((1,), (1,)), ((), ())),
-        preferred_element_type=jnp.float32,
-    ).reshape(low_terms.shape)
-
     pl.semaphore_wait(barrier, 2 * (GROUP - 1))
 
     def piece(t):
-        number = t // 4 * 2 + lax.rem(t, 2)
+        number = lax.rem(t // 4, 2) * 4 + lax.rem(t, 2) * 2 + lax.rem(t // 2, 2)
         return pl.ds(pl.multiple_of(number * PIECE, PIECE), PIECE)
 
+    def both(t):
+        number = lax.rem(t // 4, 2) * 2 + lax.rem(t, 2)
+        return pl.ds(pl.multiple_of(number * 2 * PIECE, 2 * PIECE), 2 * PIECE)
+
+    side = me_t // RING
+
     def plane_copy(step, source):
-        t = lax.rem(me_t + step, GROUP)
+        t = side * RING + lax.rem(me_t + step, RING)
         return remote(
             attention.at[piece(t), :],
-            middle.at[lax.rem(source, RING), source // RING],
+            middle.at[source],
             plane_send.at[step],
             plane_recv.at[source],
             (me_d, t),
         )
 
-    each_other(lambda step: plane_copy(step, me_t).start())
-    middle[lax.rem(me_t, RING), me_t // RING] = attention[piece(me_t), :]
+    own_place = lax.rem(me_t, RING)
+    for step in range(1, RING):
+        plane_copy(step, own_place).start()
+    middle[own_place] = attention[piece(me_t), :]
 
     def weight_copy(chunk, slot):
         place = pl.ds(chunk * CHUNK, CHUNK)
@@ -190,7 +193,7 @@
             (lax.rem(me_d + RING, GROUP), me_t),
         )
 
-    for chunk in range(chunks):
+    for chunk in range(chunks // 2):
         weight_copy(chunk, half).start()
 
     def add_rows(terms, slots, total, sems):
@@ -233,39 +236,21 @@
 
     low_begin, low_middle, low_end = add_rows(low_terms, low_slots, low_all, low_sems)
     back_begin, back_middle, back_end = add_rows(back_terms, back_slots, back_all, back_sems)
-    low_begin()
 
     def at_y(shift):
         return lax.rem(me_t + (shift % 4) * 4, GROUP)
 
     other = me_t + 1 - 2 * core
+    across = me_t + 2 - 4 * lax.rem(me_t // 2, 2)
 
     def z_of(number):
         return lax.rem(me_z + NEAR[number] + RING, RING)
 
-    def y_copy(number, way, owner):
-        part = tokens.at[z_of(number), :, piece(owner), :]
-        return remote(
-            part, part, y_send.at[number, way], y_recv.at[number, way], (me_d, at_y((1, -1)[way]))
-        )
-
-    def f_copy(number, way, owner):
-        part = tokens.at[z_of(number), way, piece(owner), :]
-        return remote(
-            part, part, f_send.at[number, way], f_recv.at[number, way], (me_d, at_y((1, -1)[way]))
-        )
-
-    def core_copy(number, shift, owner):
-        part = tokens.at[z_of(number), :, piece(owner), :]
-        return remote(
-            part, part, core_send.at[number, shift], core_recv.at[number, shift], (me_d, other)
-        )
-
     def z_copy(number, source):
         goal = z_of(number)
         return remote(
             middle.at[goal],
-            tokens.at[source, :, piece(me_t), :],
+            tokens.at[source, side, piece(me_t), :],
             z_send.at[number],
             z_recv.at[source],
             (half * RING + goal, me_t),
@@ -273,32 +258,69 @@
 
     def along_z(number):
         goal = z_of(number)
-        for h in range(2):
-            source = goal + h * RING
-            pl.when(source != me_t)(plane_copy(1, source).wait_recv)
+        pl.when(goal != own_place)(plane_copy(1, goal).wait_recv)
         if NEAR[number] == 0:
-            tokens[me_z, :, piece(me_t), :] = middle[me_z]
+            tokens[me_z, side, piece(me_t), :] = middle[me_z]
         else:
             z_copy(number, me_z).start()
 
-    def spread_own(number):
+    def x_copy(number, owner):
+        part = tokens.at[z_of(number), side, piece(owner), :]
+        return remote(part, part, x_send.at[number], x_recv.at[number], (me_d, across))
+
+    def y_copy(number, way, owner):
+        part = tokens.at[z_of(number), owner // RING, both(owner), :]
+        return remote(
+            part,
+            part,
+            y_send.at[number, way],
+            y_recv.at[number, way],
+            (me_d, at_y((1, -1, 2)[way])),
+        )
+
+    def f_copy(number, way, owner):
+        start = lax.rem(owner // 4, 2) * 4 + lax.rem(owner, 2) * 2 + way
+        place = pl.ds(pl.multiple_of(start * PIECE, PIECE), PIECE)
+        part = tokens.at[z_of(number), owner // RING, place, :]
+        return remote(
+            part, part, f_send.at[number, way], f_recv.at[number, way], (me_d, at_y((1, -1)[way]))
+        )
+
+    def core_copy(number, shift, owner):
+        part = tokens.at[z_of(number), owner // RING, both(owner), :]
+        return remote(
+            part, part, core_send.at[number, shift], core_recv.at[number, shift], (me_d, other)
+        )
+
+    def over_x(number):
         if NEAR[number] != 0:
             z_copy(number, z_of(number)).wait_recv()
+        x_copy(number, me_t).start()
+
+    def spread_own(number):
+        x_copy(number, across).wait_recv()
         y_copy(number, 0, me_t).start()
         y_copy(number, 1, me_t).start()
+        if number < DIRECT:
+            y_copy(number, 2, me_t).start()
         core_copy(number, 0, me_t).start()
 
     def spread_next(number):
         y_copy(number, 0, at_y(-1)).wait_recv()
-        f_copy(number, 0, at_y(-1)).start()
+        if number >= DIRECT:
+            f_copy(number, 0, at_y(-1)).start()
         core_copy(number, 3, at_y(-1)).start()
         y_copy(number, 1, at_y(1)).wait_recv()
-        f_copy(number, 1, at_y(1)).start()
+        if number >= DIRECT:
+            f_copy(number, 1, at_y(1)).start()
         core_copy(number, 1, at_y(1)).start()
 
     def spread_last(number):
-        f_copy(number, 0, at_y(2)).wait_recv()
-        f_copy(number, 1, at_y(2)).wait_recv()
+        if number < DIRECT:
+            y_copy(number, 2, at_y(2)).wait_recv()
+        else:
+            f_copy(number, 0, at_y(2)).wait_recv()
+            f_copy(number, 1, at_y(2)).wait_recv()
         core_copy(number, 2, at_y(2)).start()
 
     def arrived(number):
@@ -384,36 +406,54 @@
 
     for number in range(RING):
         along_z(number)
+    over_x(0)
+    over_x(1)
+    over_x(2)
     spread_own(0)
+    over_x(3)
+    over_x(4)
     spread_own(1)
+    over_x(5)
+    spread_next(0)
     spread_own(2)
-    spread_next(0)
-    spread_own(3)
+    over_x(6)
+    over_x(7)
     spread_next(1)
     spread_last(0)
-    spread_own(4)
-    spread_next(2)
-    spread_last(1)
+    spread_own(3)
     load(1).wait()
     for chunk in range(chunks // 2):
         weight_copy(chunk, 1 - half).wait_recv()
     arrived(0)
     send_products(4, 0)
-    spread_own(5)
+    for chunk in range(chunks // 2, chunks):
+        weight_copy(chunk, half).start()
+    spread_next(2)
+    spread_last(1)
+    spread_own(4)
     spread_next(3)
     spread_last(2)
     arrived(1)
     arrived(2)
     send_products(3, 0)
-    spread_own(6)
+    load(0).wait()
+    low_terms[...] = lax.dot_general(
+        attention[...],
+        down[...].reshape(ADAPTER_COUNT * ADAPTER_RANK, features),
+        (((1,), (1,)), ((), ())),
+        preferred_element_type=jnp.float32,
+    ).reshape(low_terms.shape)
+    low_begin()
+    spread_own(5)
     spread_next(4)
     spread_last(3)
-    spread_own(7)
+    spread_own(6)
     spread_next(5)
     spread_last(4)
     arrived(3)
     arrived(4)
     send_products(2, 0)
+    spread_own(7)
     spread_next(6)
     spread_last(5)
     spread_next(7)
@@ -529,15 +569,21 @@
 
     finish(square_b, slots_b, b_send, b_recv, out_b)
 
-    each_other(lambda step: plane_copy(step, me_t).wait_send())
+    for step in range(1, RING):
+        plane_copy(step, own_place).wait_send()
     for number in range(RING - 1):
         z_copy(number, me_z).wait_send()
     for chunk in range(chunks):
         weight_copy(chunk, half).wait_send()
     for number in range(RING):
+        x_copy(number, me_t).wait_send()
         for way in range(2):
             y_copy(number, way, me_t).wait_send()
-            f_copy(number, way, me_t).wait_send()
+        if number < DIRECT:
+            y_copy(number, 2, me_t).wait_send()
+        else:
+            for way in range(2):
+                f_copy(number, way, me_t).wait_send()
         for shift in range(4):
             core_copy(number, shift, me_t).wait_send()
 
@@ -581,7 +627,7 @@
         in_specs=[pl.BlockSpec(memory_space=pltpu.SMEM), vmem, vmem] + [hbm] * 5,
         out_specs=(vmem, vmem),
         scratch_shapes=[
-            pltpu.VMEM((RING, 2, PIECE, features), bf16),
+            pltpu.VMEM((RING, PIECE, features), bf16),
             pltpu.VMEM((RING, 2, LEN, features), bf16),
             pltpu.VMEM((2, depth, columns), bf16),
             pltpu.VMEM((LEN, columns), bf16),
@@ -607,14 +653,16 @@
             pltpu.VMEM((GROUP, wide // GROUP, features), bf16),
             pltpu.VMEM((GROUP, wide // GROUP, features), bf16),
             sem((5,)),
-            sem((GROUP,)),
-            sem((GROUP,)),
+            sem((RING,)),
+            sem((RING,)),
+            sem((RING,)),
+            sem((RING,)),
             sem((RING,)),
             sem((RING,)),
             sem((chunks,)),
             sem((chunks,)),
-            sem((RING, 2)),
-            sem((RING, 2)),
+            sem((RING, 3)),
+            sem((RING, 3)),
             sem((RING, 2)),
             sem((RING, 2)),
             sem((RING, 4)),

time: 124 us -> 128 us (1.032)
  Pallas kernels: 120 us -> 124 us
    pallas_call x1, Pallas kernels: 120 us -> 124 us  [body(): pl.pallas_call(whole_kernel, name='fisher', out_shape=(jax.ShapeDtypeStru...]
where the time goes in v4:
time: 128 us; the launch traced here: 127 us
  Pallas kernels  124 us (97%)
  local copies, waits for them, and re-layouts  2.85 us (2%)
    pallas_call x1, Pallas kernels, body(): pl.pallas_call(whole_kernel, name='fisher', out_shape=(jax.ShapeDtypeStru...  124 us
    unnamed x2, local copies, waits for them, and re-layouts  2.85 us

profile of v4, /device:TPU:1, one launch (start us, length us, event | category | flops | bytes accessed | tf_op | source)
XLA Modules:
  0.0 127.4 jit_solution(3410465060257925287)
XLA Ops:
  0.6 123.9 %fisher.1 = (f32[4,4,512]{2,1,0:T(4,128)}, f32[4,4,1024]{2,1,0:T(4,128)}) custom-call(s32[4]{0:T(128)} %objective.1, f32[1,1024]{1,0:T(1,128)} %bitcast.1, bf16[256,512]{1,0:T(8,128)(2,1)} %attention.1, bf16[512,1024]{1,0:T(8,128)(2,1)} %weight_hbm.1, bf16[256,1024]{1,0:T(8,128)(2,1)} %residual_hbm.1, bf16[4,256,1024]{2,1,0:T(8,128)(2,1)} %cotangent_hbm.1, ...), custom_call_target="tpu_custom_call" | custom-call | tf_op jit(solution)/shard_map/fisher/pallas_call | solution.py:620
  124.6 1.4 %copy.12 = f32[4,4,512]{2,1,0:T(4,128)} copy(f32[4,4,512]{2,1,0:T(4,128)} %get-tuple-element.4) | data formatting | bytes 65536
  126.0 1.5 %copy.13 = f32[4,4,1024]{2,1,0:T(4,128)} copy(f32[4,4,1024]{2,1,0:T(4,128)} %get-tuple-element.5) | data formatting | bytes 131072

commit v5 on v4

--- a/solution.py
+++ b/solution.py
@@ -37,7 +37,6 @@
 NEAR = (4, 3, -3, 2, -2, 1, -1, 0)
 CHUNK = 256
 PIECE = 32
-DIRECT = 3
 
 
 def spread(picked, step):
@@ -108,8 +107,6 @@
     weight_recv,
     y_send,
     y_recv,
-    f_send,
-    f_recv,
     core_send,
     core_recv,
     ring_send,
@@ -178,11 +175,6 @@
             (me_d, t),
         )
 
-    own_place = lax.rem(me_t, RING)
-    for step in range(1, RING):
-        plane_copy(step, own_place).start()
-    middle[own_place] = attention[piece(me_t), :]
-
     def weight_copy(chunk, slot):
         place = pl.ds(chunk * CHUNK, CHUNK)
         return remote(
@@ -193,8 +185,12 @@
             (lax.rem(me_d + RING, GROUP), me_t),
         )
 
-    for chunk in range(chunks // 2):
-        weight_copy(chunk, half).start()
+    own_place = lax.rem(me_t, RING)
+    for step in range(1, RING):
+        plane_copy(step, own_place).start()
+    middle[own_place] = attention[piece(me_t), :]
+
+    weight_copy(0, half).start()
 
     def add_rows(terms, slots, total, sems):
         def term_copy(step):
@@ -278,14 +274,6 @@
             (me_d, at_y((1, -1, 2)[way])),
         )
 
-    def f_copy(number, way, owner):
-        start = lax.rem(owner // 4, 2) * 4 + lax.rem(owner, 2) * 2 + way
-        place = pl.ds(pl.multiple_of(start * PIECE, PIECE), PIECE)
-        part = tokens.at[z_of(number), owner // RING, place, :]
-        return remote(
-            part, part, f_send.at[number, way], f_recv.at[number, way], (me_d, at_y((1, -1)[way]))
-        )
-
     def core_copy(number, shift, owner):
         part = tokens.at[z_of(number), owner // RING, both(owner), :]
         return remote(
@@ -299,29 +287,15 @@
 
     def spread_own(number):
         x_copy(number, across).wait_recv()
+        y_copy(number, 2, me_t).start()
         y_copy(number, 0, me_t).start()
         y_copy(number, 1, me_t).start()
-        if number < DIRECT:
-            y_copy(number, 2, me_t).start()
         core_copy(number, 0, me_t).start()
 
-    def spread_next(number):
-        y_copy(number, 0, at_y(-1)).wait_recv()
-        if number >= DIRECT:
-            f_copy(number, 0, at_y(-1)).start()
-        core_copy(number, 3, at_y(-1)).start()
-        y_copy(number, 1, at_y(1)).wait_recv()
-        if number >= DIRECT:
-            f_copy(number, 1, at_y(1)).start()
-        core_copy(number, 1, at_y(1)).start()
-
-    def spread_last(number):
-        if number < DIRECT:
-            y_copy(number, 2, at_y(2)).wait_recv()
-        else:
-            f_copy(number, 0, at_y(2)).wait_recv()
-            f_copy(number, 1, at_y(2)).wait_recv()
-        core_copy(number, 2, at_y(2)).start()
+    def pass_on(number):
+        for way, shift in ((0, -1), (1, 1), (2, 2)):
+            y_copy(number, way, at_y(shift)).wait_recv()
+            core_copy(number, shift % 4, at_y(shift)).start()
 
     def arrived(number):
         for shift in range(4):
@@ -335,7 +309,7 @@
             tokens[z, 1], weight[1, :, cols], preferred_element_type=jnp.float32
         )
 
-    def ring_copy(way, far, chunk, slot):
+    def ring_copy(way, far, chunk):
         if far == 4:
             place = pl.ds(way * (LEN // 2), LEN // 2)
         else:
@@ -350,92 +324,91 @@
         )
 
     def cols_of(chunk):
-        return pl.ds(pl.multiple_of(chunk * CHUNK, CHUNK), CHUNK)
-
-    def send_products(far, begin):
-        def one(chunk, carry):
-            cols = cols_of(chunk)
-            if far == 4:
-                value = product(0, cols).astype(jnp.bfloat16)
-                for way in range(2):
-                    mine = slice(way * (LEN // 2), (way + 1) * (LEN // 2))
-                    ring_out[way, 3, chunk, mine, :] = value[mine]
-                    ring_copy(way, 4, chunk, 0).start()
-                return carry
+        return pl.ds(chunk * CHUNK, CHUNK)
+
+    def send_products(far, chunk):
+        cols = cols_of(chunk)
+        if far == 4:
+            value = product(0, cols).astype(jnp.bfloat16)
             for way in range(2):
-                number = NEAR.index((far, -far)[way])
-                value = product(number, cols)
-                ring_copy(way, far + 1, chunk, 0).wait_recv()
-                if far == 3:
-                    mine = slice(way * (LEN // 2), (way + 1) * (LEN // 2))
-                    rest = slice((1 - way) * (LEN // 2), (2 - way) * (LEN // 2))
-                    ring_out[way, 2, chunk, mine, :] = (
-                        value[mine] + ring_in[way, 3, chunk, mine, :].astype(jnp.float32)
-                    ).astype(jnp.bfloat16)
-                    ring_out[way, 2, chunk, rest, :] = value[rest].astype(jnp.bfloat16)
-                else:
-                    ring_out[way, far - 1, chunk] = (
-                        value + ring_in[way, far, chunk].astype(jnp.float32)
-                    ).astype(jnp.bfloat16)
-                ring_copy(way, far, chunk, 0).start()
-            return carry
-
-        lax.fori_loop(begin, begin + chunks // 2, one, 0)
-
-    def own_products(begin):
-        def one(chunk, carry):
-            cols = cols_of(chunk)
-            value = product(NEAR.index(0), cols)
-            for way in range(2):
-                ring_copy(way, 1, chunk, 0).wait_recv()
-                value = value + ring_in[way, 0, chunk].astype(jnp.float32)
-            value = value + residual[:, cols].astype(jnp.float32)
-            for step in range(PASSES):
-                here = value + jnp.dot(
-                    low_wide[step], up_wide[step, :, cols], preferred_element_type=jnp.float32
-                )
-                hidden[step, :, cols] = here
-                weighted = cotangent[step, :, cols].astype(jnp.float32) * scale[:, cols]
-                squares = here * here
-                inner = weighted * here
-                sums[2 * step] += squares[:, :128] + squares[:, 128:]
-                sums[2 * step + 1] += inner[:, :128] + inner[:, 128:]
-            return carry
-
-        lax.fori_loop(begin, begin + chunks // 2, one, 0)
-
-    for number in range(RING):
-        along_z(number)
+                mine = slice(way * (LEN // 2), (way + 1) * (LEN // 2))
+                ring_out[way, 3, chunk, mine, :] = value[mine]
+                ring_copy(way, 4, chunk).start()
+            return
+        for way in range(2):
+            value = product(NEAR.index((far, -far)[way]), cols)
+            ring_copy(way, far + 1, chunk).wait_recv()
+            if far == 3:
+                mine = slice(way * (LEN // 2), (way + 1) * (LEN // 2))
+                rest = slice((1 - way) * (LEN // 2), (2 - way) * (LEN // 2))
+                ring_out[way, 2, chunk, mine, :] = (
+                    value[mine] + ring_in[way, 3, chunk, mine, :].astype(jnp.float32)
+                ).astype(jnp.bfloat16)
+                ring_out[way, 2, chunk, rest, :] = value[rest].astype(jnp.bfloat16)
+            else:
+                ring_out[way, far - 1, chunk] = (
+                    value + ring_in[way, far, chunk].astype(jnp.float32)
+                ).astype(jnp.bfloat16)
+            ring_copy(way, far, chunk).start()
+
+    def own_products(chunk):
+        cols = cols_of(chunk)
+        value = product(NEAR.index(0), cols)
+        for way in range(2):
+            ring_copy(way, 1, chunk).wait_recv()
+            value = value + ring_in[way, 0, chunk].astype(jnp.float32)
+        value = value + residual[:, cols].astype(jnp.float32)
+        for step in range(PASSES):
+            here = value + jnp.dot(
+                low_wide[step], up_wide[step, :, cols], preferred_element_type=jnp.float32
+            )
+            hidden[step, :, cols] = here
+            weighted = cotangent[step, :, cols].astype(jnp.float32) * scale[:, cols]
+            squares = here * here
+            inner = weighted * here
+            sums[2 * step] += squares[:, :128] + squares[:, 128:]
+            sums[2 * step + 1] += inner[:, :128] + inner[:, 128:]
+
+    along_z(0)
+    along_z(1)
+    along_z(2)
+    along_z(3)
+    along_z(4)
+    along_z(5)
+    along_z(6)
+    along_z(7)
     over_x(0)
     over_x(1)
     over_x(2)
-    spread_own(0)
     over_x(3)
     over_x(4)
-    spread_own(1)
     over_x(5)
-    spread_next(0)
-    spread_own(2)
     over_x(6)
     over_x(7)
-    spread_next(1)
-    spread_last(0)
+    weight_copy(1, half).start()
+    spread_own(0)
+    spread_own(1)
+    spread_own(2)
     spread_own(3)
+    spread_own(4)
+    spread_own(5)
+    spread_own(6)
+    spread_own(7)
+    weight_copy(2, half).start()
+    weight_copy(3, half).start()
+    pass_on(0)
     load(1).wait()
-    for chunk in range(chunks // 2):
-        weight_copy(chunk, 1 - half).wait_recv()
+    weight_copy(0, 1 - half).wait_recv()
     arrived(0)
     send_products(4, 0)
-    for chunk in range(chunks // 2, chunks):
-        weight_copy(chunk, half).start()
-    spread_next(2)
-    spread_last(1)
-    spread_own(4)
-    spread_next(3)
-    spread_last(2)
+    weight_copy(1, 1 - half).wait_recv()
+    send_products(4, 1)
+    pass_on(1)
+    pass_on(2)
     arrived(1)
     arrived(2)
     send_products(3, 0)
+    send_products(3, 1)
     load(0).wait()
     low_terms[...] = lax.dot_general(
         attention[...],
@@ -444,30 +417,26 @@
         preferred_element_type=jnp.float32,
     ).reshape(low_terms.shape)
     low_begin()
-    spread_own(5)
-    spread_next(4)
-    spread_last(3)
-    spread_own(6)
-    spread_next(5)
-    spread_last(4)
+    pass_on(3)
+    pass_on(4)
     arrived(3)
     arrived(4)
     send_products(2, 0)
-    spread_own(7)
-    spread_next(6)
-    spread_last(5)
-    spread_next(7)
-    spread_last(6)
+    send_products(2, 1)
+    weight_copy(2, 1 - half).wait_recv()
+    weight_copy(3, 1 - half).wait_recv()
+    send_products(4, 2)
+    send_products(4, 3)
+    pass_on(5)
+    pass_on(6)
     arrived(5)
     arrived(6)
     send_products(1, 0)
-    spread_last(7)
-    arrived(7)
-    for chunk in range(chunks // 2, chunks):
-        weight_copy(chunk, 1 - half).wait_recv()
-    send_products(4, chunks // 2)
+    send_products(1, 1)
     low_middle()
-    send_products(3, chunks // 2)
+    pass_on(7)
+    send_products(3, 2)
+    send_products(3, 3)
     low_end()
     for number in range(2, 5):
         load(number).wait()
@@ -481,10 +450,15 @@
             choice, up_rows, (((0,), (0,)), ((), ())), preferred_element_type=jnp.float32
         ).astype(jnp.bfloat16)
     sums[...] = jnp.zeros(sums.shape, jnp.float32)
-    send_products(2, chunks // 2)
+    arrived(7)
     own_products(0)
-    send_products(1, chunks // 2)
-    own_products(chunks // 2)
+    own_products(1)
+    send_products(2, 2)
+    send_products(2, 3)
+    send_products(1, 2)
+    send_products(1, 3)
+    own_products(2)
+    own_products(3)
 
     lane = lax.broadcasted_iota(jnp.int32, (LEN, 128), 1)
     stats = jnp.zeros((LEN, 128), jnp.float32)
@@ -577,20 +551,15 @@
         weight_copy(chunk, half).wait_send()
     for number in range(RING):
         x_copy(number, me_t).wait_send()
-        for way in range(2):
+        for way in range(3):
             y_copy(number, way, me_t).wait_send()
-        if number < DIRECT:
-            y_copy(number, 2, me_t).wait_send()
-        else:
-            for way in range(2):
-                f_copy(number, way, me_t).wait_send()
         for shift in range(4):
             core_copy(number, shift, me_t).wait_send()
 
     def ring_done(chunk, carry):
         for way in range(2):
             for far in range(1, 5):
-                ring_copy(way, far, chunk, 0).wait_send()
+                ring_copy(way, far, chunk).wait_send()
         return carry
 
     lax.fori_loop(0, chunks, ring_done, 0)
@@ -663,8 +632,6 @@
             sem((chunks,)),
             sem((RING, 3)),
             sem((RING, 3)),
-            sem((RING, 2)),
-            sem((RING, 2)),
             sem((RING, 4)),
             sem((RING, 4)),
             sem((2, 4, chunks)),

time: 128 us -> 117 us (0.914)
  Pallas kernels: 124 us -> 113 us
    pallas_call x1, Pallas kernels: 124 us -> 113 us  [body(): pl.pallas_call(whole_kernel, name='fisher', out_shape=(jax.ShapeDtypeStru...]
where the time goes in v5:
time: 117 us
  Pallas kernels  113 us (97%)
  local copies, waits for them, and re-layouts  2.85 us (2%)
    pallas_call x1, Pallas kernels, body(): pl.pallas_call(whole_kernel, name='fisher', out_shape=(jax.ShapeDtypeStru...  113 us
    unnamed x2, local copies, waits for them, and re-layouts  2.85 us

profile of v5, /device:TPU:1, one launch (start us, length us, event | category | flops | bytes accessed | tf_op | source)
XLA Modules:
  0.0 116.9 jit_solution(4171746127437715406)
XLA Ops:
  0.6 113.5 %fisher.1 = (f32[4,4,512]{2,1,0:T(4,128)}, f32[4,4,1024]{2,1,0:T(4,128)}) custom-call(s32[4]{0:T(128)} %objective.1, f32[1,1024]{1,0:T(1,128)} %bitcast.1, bf16[256,512]{1,0:T(8,128)(2,1)} %attention.1, bf16[512,1024]{1,0:T(8,128)(2,1)} %weight_hbm.1, bf16[256,1024]{1,0:T(8,128)(2,1)} %residual_hbm.1, bf16[4,256,1024]{2,1,0:T(8,128)(2,1)} %cotangent_hbm.1, ...), custom_call_target="tpu_custom_call" | custom-call | tf_op jit(solution)/shard_map/fisher/pallas_call | solution.py:589
  114.1 1.4 %copy.12 = f32[4,4,512]{2,1,0:T(4,128)} copy(f32[4,4,512]{2,1,0:T(4,128)} %get-tuple-element.4) | data formatting | bytes 65536
  115.5 1.5 %copy.13 = f32[4,4,1024]{2,1,0:T(4,128)} copy(f32[4,4,1024]{2,1,0:T(4,128)} %get-tuple-element.5) | data formatting | bytes 131072

commit v6 on v5

--- a/solution.py
+++ b/solution.py
@@ -17,23 +17,8 @@
 epsilon = 1e-05
 
 
-def to_tensor(step):
-    return (lax.axis_index("dp"), lax.rem(lax.axis_index("tensor") + step, GROUP))
-
-
-def to_dp(step):
-    return (lax.rem(lax.axis_index("dp") + step, GROUP), lax.axis_index("tensor"))
-
-
-def each_other(action):
-    def one(step, carry):
-        action(step)
-        return carry
-
-    lax.fori_loop(1, GROUP, one, 0)
-
-
 RING = 8
+CHIPS = 8
 NEAR = (4, 3, -3, 2, -2, 1, -1, 0)
 CHUNK = 256
 PIECE = 32
@@ -84,17 +69,22 @@
     sums,
     grads,
     low_terms,
+    low_pair,
     low_slots,
     low_all,
     low_wide,
     up_wide,
+    stat_own,
     stat_slots,
     back_terms,
+    back_pair,
     back_slots,
     back_all,
     square_b,
+    from_x_b,
     slots_b,
     square_a,
+    from_x_a,
     slots_a,
     local,
     plane_send,
@@ -115,10 +105,10 @@
     back_sems,
     stat_send,
     stat_recv,
-    b_send,
-    b_recv,
-    a_send,
-    a_recv,
+    bx_sems,
+    bz_sems,
+    ax_sems,
+    az_sems,
 ):
     me_d = lax.axis_index("dp")
     me_t = lax.axis_index("tensor")
@@ -133,11 +123,28 @@
 
     barrier = pltpu.get_barrier_semaphore()
 
-    def greet(step):
-        pl.semaphore_signal(barrier, inc=1, device_id=to_tensor(step), device_id_type=MESH)
-        pl.semaphore_signal(barrier, inc=1, device_id=to_dp(step), device_id_type=MESH)
-
-    each_other(greet)
+    chip = me_t // 2
+    other = me_t + 1 - 2 * core
+
+    def same_core(step):
+        return (me_d, lax.rem(chip + step, CHIPS) * 2 + core)
+
+    def at_z(step):
+        return (half * RING + lax.rem(me_z + step, RING), me_t)
+
+    beside = (lax.rem(me_d + RING, GROUP), me_t)
+
+    def greet(device):
+        pl.semaphore_signal(barrier, inc=1, device_id=device, device_id_type=MESH)
+
+    greet((me_d, other))
+    greet(beside)
+    for step in range(1, 4):
+        greet((me_d, (chip // 4 * 4 + lax.rem(chip + step, 4)) * 2 + 1 - core))
+    for step in range(1, CHIPS):
+        greet(same_core(step))
+    for step in range(1, RING):
+        greet(at_z(step))
 
     def load(number):
         place = pl.ds(pl.multiple_of(me_t * features, features), features)
@@ -153,7 +160,7 @@
     for number in range(5):
         load(number).start()
 
-    pl.semaphore_wait(barrier, 2 * (GROUP - 1))
+    pl.semaphore_wait(barrier, 5 + CHIPS - 1 + RING - 1)
 
     def piece(t):
         number = lax.rem(t // 4, 2) * 4 + lax.rem(t, 2) * 2 + lax.rem(t // 2, 2)
@@ -182,7 +189,7 @@
             weight.at[slot, :, place],
             weight_send.at[chunk],
             weight_recv.at[chunk],
-            (lax.rem(me_d + RING, GROUP), me_t),
+            beside,
         )
 
     own_place = lax.rem(me_t, RING)
@@ -192,51 +199,66 @@
 
     weight_copy(0, half).start()
 
-    def add_rows(terms, slots, total, sems):
+    def add_rows(terms, pair, slots, total, sems):
+        def pair_copy(part):
+            return remote(terms.at[part], pair, sems.at[0, 0], sems.at[1, 0], (me_d, other))
+
         def term_copy(step):
             return remote(
-                terms.at[lax.rem(me_t + step, GROUP)],
+                terms.at[core, lax.rem(chip + step, CHIPS)],
                 slots.at[step],
                 sems.at[0, step],
                 sems.at[1, step],
-                to_tensor(step),
+                same_core(step),
             )
 
         def full_copy(step, owner):
-            place = pl.ds(pl.multiple_of(owner * rows, rows), rows)
+            part = total.at[core, owner]
+            return remote(part, part, sems.at[2, step], sems.at[3, step], same_core(step))
+
+        def last_copy(part):
             return remote(
-                total.at[place, :],
-                total.at[place, :],
-                sems.at[2, step],
-                sems.at[3, step],
-                to_tensor(step),
+                total.at[part], total.at[part], sems.at[2, 0], sems.at[3, 0], (me_d, other)
             )
 
         def begin():
-            each_other(lambda step: term_copy(step).start())
+            pair_copy(1 - core).start()
+
+        def second():
+            pair_copy(1 - core).wait()
+            terms[core] = terms[core] + pair[...]
+            for step in range(1, CHIPS):
+                term_copy(step).start()
 
         def middle():
-            each_other(lambda step: term_copy(step).wait())
-            slots[0] = terms[me_t]
-            mine = pl.ds(pl.multiple_of(me_t * rows, rows), rows)
-            total[mine, :] = jnp.sum(slots[...], axis=0).astype(jnp.bfloat16)
-            each_other(lambda step: full_copy(step, me_t).start())
+            for step in range(1, CHIPS):
+                term_copy(step).wait()
+            slots[0] = terms[core, chip]
+            total[core, chip] = jnp.sum(slots[...], axis=0).astype(jnp.bfloat16)
+            for step in range(1, CHIPS):
+                full_copy(step, chip).start()
 
         def end():
-            each_other(lambda step: full_copy(step, me_t).wait_send())
-            each_other(
-                lambda step: full_copy(step, lax.rem(me_t + GROUP - step, GROUP)).wait_recv()
-            )
-
-        return begin, middle, end
-
-    low_begin, low_middle, low_end = add_rows(low_terms, low_slots, low_all, low_sems)
-    back_begin, back_middle, back_end = add_rows(back_terms, back_slots, back_all, back_sems)
+            for step in range(1, CHIPS):
+                full_copy(step, chip).wait_send()
+            for step in range(1, CHIPS):
+                full_copy(step, lax.rem(chip + CHIPS - step, CHIPS)).wait_recv()
+            last_copy(core).start()
+            last_copy(core).wait_send()
+            last_copy(1 - core).wait_recv()
+
+        return begin, second, middle, end
+
+    low_begin, low_second, low_middle, low_end = add_rows(
+        low_terms, low_pair, low_slots, low_all, low_sems
+    )
+    back_begin, back_second, back_middle, back_end = add_rows(
+        back_terms, back_pair, back_slots, back_all, back_sems
+    )
 
     def at_y(shift):
         return lax.rem(me_t + (shift % 4) * 4, GROUP)
 
-    other = me_t + 1 - 2 * core
     across = me_t + 2 - 4 * lax.rem(me_t // 2, 2)
 
     def z_of(number):
@@ -419,6 +441,7 @@
     low_begin()
     pass_on(3)
     pass_on(4)
+    low_second()
     arrived(3)
     arrived(4)
     send_products(2, 0)
@@ -440,11 +463,12 @@
     low_end()
     for number in range(2, 5):
         load(number).wait()
+    low_rows = low_all[...].reshape(LEN, wide)
     up_rows = up[...].reshape(ADAPTER_COUNT * ADAPTER_RANK, columns)
     for step in range(PASSES):
         choice = spread(objective[step], step)
         low_wide[step] = jnp.dot(
-            low_all[...], choice, preferred_element_type=jnp.float32
+            low_rows, choice, preferred_element_type=jnp.float32
         ).astype(jnp.bfloat16)
         up_wide[step] = lax.dot_general(
             choice, up_rows, (((0,), (0,)), ((), ())), preferred_element_type=jnp.float32
@@ -464,7 +488,12 @@
     stats = jnp.zeros((LEN, 128), jnp.float32)
     for kind in range(2 * PASSES):
         stats = jnp.where(lane == kind, jnp.sum(sums[kind], axis=1, keepdims=True), stats)
-    stat_slots[0] = stats.T[: 2 * PASSES]
+    stat_own[0] = stats.T[: 2 * PASSES]
+
+    def stat_pair():
+        return remote(
+            stat_own.at[0], stat_own.at[1], stat_send.at[0], stat_recv.at[0], (me_d, other)
+        )
 
     def stat_copy(step):
         return remote(
@@ -472,11 +501,16 @@
             stat_slots.at[step],
             stat_send.at[step],
             stat_recv.at[step],
-            to_tensor(step),
-        )
-
-    each_other(lambda step: stat_copy(step).start())
-    each_other(lambda step: stat_copy(step).wait())
+            same_core(step),
+        )
+
+    stat_pair().start()
+    stat_pair().wait()
+    stat_slots[0] = stat_own[0] + stat_own[1]
+    for step in range(1, CHIPS):
+        stat_copy(step).start()
+    for step in range(1, CHIPS):
+        stat_copy(step).wait()
     totals = jnp.sum(stat_slots[...], axis=0)
     inner_first = jnp.concatenate([totals[1:], totals[:1]], axis=0)
     scale_inv = lax.rsqrt(totals / MODEL_WIDTH + epsilon)
@@ -508,40 +542,69 @@
         per_b = term if per_b is None else per_b + term
     square_b[...] = (per_b * per_b).astype(jnp.bfloat16).reshape(square_b.shape)
 
-    def owner_copy(step, squares, slots, send, recv):
-        return remote(
-            squares.at[lax.rem(me_d + step, GROUP)],
-            slots.at[step],
-            send.at[step],
-            recv.at[step],
-            to_dp(step),
-        )
-
-    each_other(lambda step: owner_copy(step, square_b, slots_b, b_send, b_recv).start())
-
+    def owners(squares, from_x, slots, x_sems, z_sems):
+        def x_part(number):
+            place = z_of(number)
+            return remote(
+                squares.at[1 - half, place],
+                from_x.at[place],
+                x_sems.at[0, number],
+                x_sems.at[1, number],
+                beside,
+            )
+
+        def z_part(number):
+            return remote(
+                squares.at[half, z_of(number)],
+                slots.at[number],
+                z_sems.at[0, number],
+                z_sems.at[1, number],
+                (half * RING + z_of(number), me_t),
+            )
+
+        def begin():
+            for number in range(RING):
+                x_part(number).start()
+
+        def middle():
+            for number in range(RING):
+                x_part(number).wait_recv()
+                place = z_of(number)
+                total = squares[half, place].astype(jnp.float32) + from_x[place].astype(jnp.float32)
+                if NEAR[number] == 0:
+                    slots[number] = total.astype(jnp.bfloat16)
+                else:
+                    squares[half, place] = total.astype(jnp.bfloat16)
+                    z_part(number).start()
+
+        def end(out):
+            for number in range(RING):
+                if NEAR[number] != 0:
+                    z_part(number).wait_recv()
+            out[...] = jnp.sum(slots[...].astype(jnp.float32), axis=0)
+
+        def drain():
+            for number in range(RING):
+                x_part(number).wait_send()
+                if NEAR[number] != 0:
+                    z_part(number).wait_send()
+
+        return begin, middle, end, drain
+
+    b_begin, b_middle, b_end, b_drain = owners(square_b, from_x_b, slots_b, bx_sems, bz_sems)
+    a_begin, a_middle, a_end, a_drain = owners(square_a, from_x_a, slots_a, ax_sems, az_sems)
+    b_begin()
+    back_second()
     back_middle()
+    b_middle()
     back_end()
     per_a = lax.dot_general(
-        back_all[...], attention[...], (((0,), (0,)), ((), ())), preferred_element_type=jnp.float32
+        back_all[...].reshape(LEN, wide), attention[...], (((0,), (0,)), ((), ())), preferred_element_type=jnp.float32
     )
     square_a[...] = (per_a * per_a).astype(jnp.bfloat16).reshape(square_a.shape)
-    each_other(lambda step: owner_copy(step, square_a, slots_a, a_send, a_recv).start())
-
-    per = ADAPTER_RANK // GROUP
-
-    def finish(squares, slots, send, recv, out):
-        each_other(lambda step: owner_copy(step, squares, slots, send, recv).wait())
-        slots[0] = squares[me_d]
-        total = jnp.sum(slots[...].astype(jnp.float32), axis=0)
-        for adapter in range(ADAPTER_COUNT):
-            chosen = None
-            for step in range(PASSES):
-                share = jnp.where(objective[step] == adapter, 1.0 / EXAMPLES, 0.0)
-                part = share * total[step * per : (step + 1) * per]
-                chosen = part if chosen is None else chosen + part
-            out[adapter] = chosen
-
-    finish(square_b, slots_b, b_send, b_recv, out_b)
+    a_begin()
+    a_middle()
+    b_end(out_b)
 
     for step in range(1, RING):
         plane_copy(step, own_place).wait_send()
@@ -563,7 +626,9 @@
         return carry
 
     lax.fori_loop(0, chunks, ring_done, 0)
-    finish(square_a, slots_a, a_send, a_recv, out_a)
+    b_drain()
+    a_end(out_a)
+    a_drain()
 
 
 def body(
@@ -582,16 +647,17 @@
     per = ADAPTER_RANK // GROUP
     wide = PASSES * ADAPTER_RANK
     rows = LEN // GROUP
+    share = wide // GROUP
     bf16, f32 = jnp.bfloat16, jnp.float32
     vmem = pl.BlockSpec(memory_space=pltpu.VMEM)
     hbm = pl.BlockSpec(memory_space=pl.ANY)
     sem = pltpu.SemaphoreType.DMA
-    return pl.pallas_call(
+    squares = pl.pallas_call(
         whole_kernel,
         name="fisher",
         out_shape=(
-            jax.ShapeDtypeStruct((ADAPTER_COUNT, per, features), f32),
-            jax.ShapeDtypeStruct((ADAPTER_COUNT, per, columns), f32),
+            jax.ShapeDtypeStruct((share, features), f32),
+            jax.ShapeDtypeStruct((share, columns), f32),
         ),
         in_specs=[pl.BlockSpec(memory_space=pltpu.SMEM), vmem, vmem] + [hbm] * 5,
         out_specs=(vmem, vmem),
@@ -608,19 +674,24 @@
             pltpu.VMEM((PASSES, LEN, columns), f32),
             pltpu.VMEM((2 * PASSES, LEN, 128), f32),
             pltpu.VMEM((PASSES, LEN, columns), bf16),
-            pltpu.VMEM((GROUP, rows, wide), f32),
-            pltpu.VMEM((GROUP, rows, wide), f32),
-            pltpu.VMEM((LEN, wide), bf16),
+            pltpu.VMEM((2, CHIPS, rows, wide), f32),
+            pltpu.VMEM((CHIPS, rows, wide), f32),
+            pltpu.VMEM((CHIPS, rows, wide), f32),
+            pltpu.VMEM((2, CHIPS, rows, wide), bf16),
             pltpu.VMEM((PASSES, LEN, wide), bf16),
             pltpu.VMEM((PASSES, wide, columns), bf16),
-            pltpu.VMEM((GROUP, 2 * PASSES, LEN), f32),
-            pltpu.VMEM((GROUP, rows, wide), f32),
-            pltpu.VMEM((GROUP, rows, wide), f32),
-            pltpu.VMEM((LEN, wide), bf16),
-            pltpu.VMEM((GROUP, wide // GROUP, columns), bf16),
-            pltpu.VMEM((GROUP, wide // GROUP, columns), bf16),
-            pltpu.VMEM((GROUP, wide // GROUP, features), bf16),
-            pltpu.VMEM((GROUP, wide // GROUP, features), bf16),
+            pltpu.VMEM((2, 2 * PASSES, LEN), f32),
+            pltpu.VMEM((CHIPS, 2 * PASSES, LEN), f32),
+            pltpu.VMEM((2, CHIPS, rows, wide), f32),
+            pltpu.VMEM((CHIPS, rows, wide), f32),
+            pltpu.VMEM((CHIPS, rows, wide), f32),
+            pltpu.VMEM((2, CHIPS, rows, wide), bf16),
+            pltpu.VMEM((2, RING, share, columns), bf16),
+            pltpu.VMEM((RING, share, columns), bf16),
+            pltpu.VMEM((RING, share, columns), bf16),
+            pltpu.VMEM((2, RING, share, features), bf16),
+            pltpu.VMEM((RING, share, features), bf16),
+            pltpu.VMEM((RING, share, features), bf16),
             sem((5,)),
             sem((RING,)),
             sem((RING,)),
@@ -636,10 +707,12 @@
             sem((RING, 4)),
             sem((2, 4, chunks)),
             sem((2, 4, chunks)),
-            sem((4, GROUP)),
-            sem((4, GROUP)),
+            sem((4, CHIPS)),
+            sem((4, CHIPS)),
+            sem((CHIPS,)),
+            sem((CHIPS,)),
         ]
-        + [sem((GROUP,))] * 6,
+        + [sem((2, RING))] * 4,
         compiler_params=pltpu.CompilerParams(
             collective_id=0, has_side_effects=True, vmem_limit_bytes=56 * 2**20
         ),
@@ -653,6 +726,12 @@
         adapter_down_weights,
         adapter_up_weights,
     )
+    chosen = objective[:, None] == jnp.arange(ADAPTER_COUNT, dtype=jnp.int32)[None, :]
+    weights = jnp.where(chosen, 1.0 / EXAMPLES, 0.0)[:, :, None, None]
+    return tuple(
+        jnp.sum(weights * total.reshape(PASSES, 1, per, total.shape[1]), axis=0)
+        for total in squares
+    )
 
 
 def solution(mesh):

time: 117 us -> 118 us (level)
  other arithmetic: 0 us -> 2.21 us
  local copies, waits for them, and re-layouts: 2.85 us -> 1.63 us
    unnamed x2 -> x0, local copies, waits for them, and re-layouts: 2.85 us -> none
    mul x0 -> x2, local copies, waits for them, and re-layouts: none -> 1.63 us  [body(): weights * total.reshape(PASSES, 1, per, total.shape[1])]
    reduce_sum x0 -> x2, other arithmetic: none -> 1.48 us  [body(): jnp.sum(weights * total.reshape(PASSES, 1, per, total.shape[1]), axis=0)]
where the time goes in v6:
time: 118 us
  Pallas kernels  114 us (97%)
  other arithmetic  2.21 us (2%)
  local copies, waits for them, and re-layouts  1.63 us (1%)
    pallas_call x1, Pallas kernels, body(): pl.pallas_call(whole_kernel, name='fisher', out_shape=(jax.ShapeDtypeStru...  114 us

profile of v6, /device:TPU:1, one launch (start us, length us, event | category | flops | bytes accessed | tf_op | source)
XLA Modules:
  0.0 118.2 jit_solution(12942354387611782866)
XLA Ops:
  0.6 0.7 fusion
  1.4 113.7 %fisher.1 = (f32[16,512]{1,0:T(8,128)}, f32[16,1024]{1,0:T(8,128)}) custom-call(s32[4]{0:T(128)} %objective.1, f32[1,1024]{1,0:T(1,128)} %bitcast.1, bf16[256,512]{1,0:T(8,128)(2,1)} %attention.1, bf16[512,1024]{1,0:T(8,128)(2,1)} %weight_hbm.1, bf16[256,1024]{1,0:T(8,128)(2,1)} %residual_hbm.1, bf16[4,256,1024]{2,1,0:T(8,128)(2,1)} %cotangent_hbm.1, ...), custom_call_target="tpu_custom_call" | custom-call | tf_op jit(solution)/shard_map/fisher/pallas_call | solution.py:655
  115.1 0.8 mul.31
  115.9 0.7 multiply_reduce_fusion.1
  116.6 0.9 mul.35
  117.4 0.8 multiply_reduce_fusion

commit v7 on v6

--- a/solution.py
+++ b/solution.py
@@ -15,6 +15,14 @@
 MESH = pl.DeviceIdType.MESH
 
 epsilon = 1e-05
+
+
+def each_other(action):
+    def one(step, carry):
+        action(step)
+        return carry
+
+    lax.fori_loop(1, GROUP, one, 0)
 
 
 RING = 8
@@ -69,7 +77,6 @@
     sums,
     grads,
     low_terms,
-    low_pair,
     low_slots,
     low_all,
     low_wide,
@@ -77,7 +84,6 @@
     stat_own,
     stat_slots,
     back_terms,
-    back_pair,
     back_slots,
     back_all,
     square_b,
@@ -137,12 +143,9 @@
     def greet(device):
         pl.semaphore_signal(barrier, inc=1, device_id=device, device_id_type=MESH)
 
-    greet((me_d, other))
     greet(beside)
-    for step in range(1, 4):
-        greet((me_d, (chip // 4 * 4 + lax.rem(chip + step, 4)) * 2 + 1 - core))
-    for step in range(1, CHIPS):
-        greet(same_core(step))
+    for step in range(1, GROUP):
+        greet((me_d, lax.rem(me_t + step, GROUP)))
     for step in range(1, RING):
         greet(at_z(step))
 
@@ -160,7 +163,7 @@
     for number in range(5):
         load(number).start()
 
-    pl.semaphore_wait(barrier, 5 + CHIPS - 1 + RING - 1)
+    pl.semaphore_wait(barrier, 1 + GROUP - 1 + RING - 1)
 
     def piece(t):
         number = lax.rem(t // 4, 2) * 4 + lax.rem(t, 2) * 2 + lax.rem(t // 2, 2)
@@ -199,62 +202,49 @@
 
     weight_copy(0, half).start()
 
-    def add_rows(terms, pair, slots, total, sems):
-        def pair_copy(part):
-            return remote(terms.at[part], pair, sems.at[0, 0], sems.at[1, 0], (me_d, other))
-
+    def in_plane(step):
+        return (me_d, lax.rem(me_t + step, GROUP))
+
+    def add_rows(terms, slots, total, sems):
         def term_copy(step):
             return remote(
-                terms.at[core, lax.rem(chip + step, CHIPS)],
+                terms.at[lax.rem(me_t + step, GROUP)],
                 slots.at[step],
                 sems.at[0, step],
                 sems.at[1, step],
-                same_core(step),
+                in_plane(step),
             )
 
         def full_copy(step, owner):
-            part = total.at[core, owner]
-            return remote(part, part, sems.at[2, step], sems.at[3, step], same_core(step))
-
-        def last_copy(part):
+            place = pl.ds(pl.multiple_of(owner * rows, rows), rows)
             return remote(
-                total.at[part], total.at[part], sems.at[2, 0], sems.at[3, 0], (me_d, other)
+                total.at[place, :],
+                total.at[place, :],
+                sems.at[2, step],
+                sems.at[3, step],
+                in_plane(step),
             )
 
         def begin():
-            pair_copy(1 - core).start()
-
-        def second():
-            pair_copy(1 - core).wait()
-            terms[core] = terms[core] + pair[...]
-            for step in range(1, CHIPS):
-                term_copy(step).start()
+            each_other(lambda step: term_copy(step).start())
 
         def middle():
-            for step in range(1, CHIPS):
-                term_copy(step).wait()
-            slots[0] = terms[core, chip]
-            total[core, chip] = jnp.sum(slots[...], axis=0).astype(jnp.bfloat16)
-            for step in range(1, CHIPS):
-                full_copy(step, chip).start()
+            each_other(lambda step: term_copy(step).wait())
+            slots[0] = terms[me_t]
+            mine = pl.ds(pl.multiple_of(me_t * rows, rows), rows)
+            total[mine, :] = jnp.sum(slots[...], axis=0).astype(jnp.bfloat16)
+            each_other(lambda step: full_copy(step, me_t).start())
 
         def end():
-            for step in range(1, CHIPS):
-                full_copy(step, chip).wait_send()
-            for step in range(1, CHIPS):
-                full_copy(step, lax.rem(chip + CHIPS - step, CHIPS)).wait_recv()
-            last_copy(core).start()
-            last_copy(core).wait_send()
-            last_copy(1 - core).wait_recv()
-
-        return begin, second, middle, end
-
-    low_begin, low_second, low_middle, low_end = add_rows(
-        low_terms, low_pair, low_slots, low_all, low_sems
-    )
-    back_begin, back_second, back_middle, back_end = add_rows(
-        back_terms, back_pair, back_slots, back_all, back_sems
-    )
+            each_other(lambda step: full_copy(step, me_t).wait_send())
+            each_other(
+                lambda step: full_copy(step, lax.rem(me_t + GROUP - step, GROUP)).wait_recv()
+            )
+
+        return begin, middle, end
+
+    low_begin, low_middle, low_end = add_rows(low_terms, low_slots, low_all, low_sems)
+    back_begin, back_middle, back_end = add_rows(back_terms, back_slots, back_all, back_sems)
 
     def at_y(shift):
         return lax.rem(me_t + (shift % 4) * 4, GROUP)
@@ -441,7 +431,6 @@
     low_begin()
     pass_on(3)
     pass_on(4)
-    low_second()
     arrived(3)
     arrived(4)
     send_products(2, 0)
@@ -463,12 +452,11 @@
     low_end()
     for number in range(2, 5):
         load(number).wait()
-    low_rows = low_all[...].reshape(LEN, wide)
     up_rows = up[...].reshape(ADAPTER_COUNT * ADAPTER_RANK, columns)
     for step in range(PASSES):
         choice = spread(objective[step], step)
         low_wide[step] = jnp.dot(
-            low_rows, choice, preferred_element_type=jnp.float32
+            low_all[...], choice, preferred_element_type=jnp.float32
         ).astype(jnp.bfloat16)
         up_wide[step] = lax.dot_general(
             choice, up_rows, (((0,), (0,)), ((), ())), preferred_element_type=jnp.float32
@@ -594,12 +582,11 @@
     b_begin, b_middle, b_end, b_drain = owners(square_b, from_x_b, slots_b, bx_sems, bz_sems)
     a_begin, a_middle, a_end, a_drain = owners(square_a, from_x_a, slots_a, ax_sems, az_sems)
     b_begin()
-    back_second()
     back_middle()
     b_middle()
     back_end()
     per_a = lax.dot_general(
-        back_all[...].reshape(LEN, wide), attention[...], (((0,), (0,)), ((), ())), preferred_element_type=jnp.float32
+        back_all[...], attention[...], (((0,), (0,)), ((), ())), preferred_element_type=jnp.float32
     )
     square_a[...] = (per_a * per_a).astype(jnp.bfloat16).reshape(square_a.shape)
     a_begin()
@@ -629,6 +616,22 @@
     b_drain()
     a_end(out_a)
     a_drain()
+
+
+def choose(objective, total, out):
+    per = ADAPTER_RANK // GROUP
+    for adapter in range(ADAPTER_COUNT):
+        chosen = None
+        for step in range(PASSES):
+            share = jnp.where(objective[step] == adapter, 1.0 / EXAMPLES, 0.0)
+            part = share * total[step * per : (step + 1) * per]
+            chosen = part if chosen is None else chosen + part
+        out[adapter] = chosen
+
+
+def choose_kernel(objective, total_a, total_b, out_a, out_b):
+    choose(objective, total_a[...], out_a)
+    choose(objective, total_b[...], out_b)
 
 
 def body(
@@ -674,18 +677,16 @@
             pltpu.VMEM((PASSES, LEN, columns), f32),
             pltpu.VMEM((2 * PASSES, LEN, 128), f32),
             pltpu.VMEM((PASSES, LEN, columns), bf16),
-            pltpu.VMEM((2, CHIPS, rows, wide), f32),
-            pltpu.VMEM((CHIPS, rows, wide), f32),
-            pltpu.VMEM((CHIPS, rows, wide), f32),
-            pltpu.VMEM((2, CHIPS, rows, wide), bf16),
+            pltpu.VMEM((GROUP, rows, wide), f32),
+            pltpu.VMEM((GROUP, rows, wide), f32),
+            pltpu.VMEM((LEN, wide), bf16),
             pltpu.VMEM((PASSES, LEN, wide), bf16),
             pltpu.VMEM((PASSES, wide, columns), bf16),
             pltpu.VMEM((2, 2 * PASSES, LEN), f32),
             pltpu.VMEM((CHIPS, 2 * PASSES, LEN), f32),
-            pltpu.VMEM((2, CHIPS, rows, wide), f32),
-            pltpu.VMEM((CHIPS, rows, wide), f32),
-            pltpu.VMEM((CHIPS, rows, wide), f32),
-            pltpu.VMEM((2, CHIPS, rows, wide), bf16),
+            pltpu.VMEM((GROUP, rows, wide), f32),
+            pltpu.VMEM((GROUP, rows, wide), f32),
+            pltpu.VMEM((LEN, wide), bf16),
             pltpu.VMEM((2, RING, share, columns), bf16),
             pltpu.VMEM((RING, share, columns), bf16),
             pltpu.VMEM((RING, share, columns), bf16),
@@ -707,8 +708,8 @@
             sem((RING, 4)),
             sem((2, 4, chunks)),
             sem((2, 4, chunks)),
-            sem((4, CHIPS)),
-            sem((4, CHIPS)),
+            sem((4, GROUP)),
+            sem((4, GROUP)),
             sem((CHIPS,)),
             sem((CHIPS,)),
         ]
@@ -726,12 +727,16 @@
         adapter_down_weights,
         adapter_up_weights,
     )
-    chosen = objective[:, None] == jnp.arange(ADAPTER_COUNT, dtype=jnp.int32)[None, :]
-    weights = jnp.where(chosen, 1.0 / EXAMPLES, 0.0)[:, :, None, None]
-    return tuple(
-        jnp.sum(weights * total.reshape(PASSES, 1, per, total.shape[1]), axis=0)
-        for total in squares
-    )
+    return pl.pallas_call(
+        choose_kernel,
+        name="choose",
+        out_shape=(
+            jax.ShapeDtypeStruct((ADAPTER_COUNT, per, features), f32),
+            jax.ShapeDtypeStruct((ADAPTER_COUNT, per, columns), f32),
+        ),
+        in_specs=[pl.BlockSpec(memory_space=pltpu.SMEM), vmem, vmem],
+        out_specs=(vmem, vmem),
+    )(objective, *squares)
 
 
 def solution(mesh):

time: 118 us -> 114 us (0.966)
  other arithmetic: 2.21 us -> 0 us
  local copies, waits for them, and re-layouts: 1.63 us -> 0 us
    pallas_call x1, Pallas kernels: 114 us -> 111 us  [body(): pl.pallas_call(whole_kernel, name='fisher', out_shape=(jax.ShapeDtypeStru...]
    mul x2 -> x0, local copies, waits for them, and re-layouts: 1.63 us -> none  [body(): weights * total.reshape(PASSES, 1, per, total.shape[1])]
    pallas_call x0 -> x1, Pallas kernels: none -> 1.57 us  [body(): pl.pallas_call(choose_kernel, name='choose', out_shape=(jax.ShapeDtypeStr...]
    reduce_sum x2 -> x0, other arithmetic: 1.48 us -> none  [body(): jnp.sum(weights * total.reshape(PASSES, 1, per, total.shape[1]), axis=0)]
where the time goes in v7:
time: 114 us
  Pallas kernels  113 us (99%)
    pallas_call x1, Pallas kernels, body(): pl.pallas_call(whole_kernel, name='fisher', out_shape=(jax.ShapeDtypeStru...  111 us

profile of v7, /device:TPU:1, one launch (start us, length us, event | category | flops | bytes accessed | tf_op | source)
XLA Modules:
  0.0 113.7 jit_solution(4151537557547723287)
XLA Ops:
  0.6 111.5 %fisher.1 = (f32[16,512]{1,0:T(8,128)}, f32[16,1024]{1,0:T(8,128)}) custom-call(s32[4]{0:T(128)} %objective.3, f32[1,1024]{1,0:T(1,128)} %bitcast.1, bf16[256,512]{1,0:T(8,128)(2,1)} %attention.1, bf16[512,1024]{1,0:T(8,128)(2,1)} %weight_hbm.1, bf16[256,1024]{1,0:T(8,128)(2,1)} %residual_hbm.1, bf16[4,256,1024]{2,1,0:T(8,128)(2,1)} %cotangent_hbm.1, ...), custom_call_target="tpu_custom_call" | custom-call | tf_op jit(solution)/shard_map/fisher/pallas_call | solution.py:658
  112.1 1.6 %choose.1 = (f32[4,4,512]{2,1,0:T(4,128)}, f32[4,4,1024]{2,1,0:T(4,128)}) custom-call(s32[4]{0:T(128)} %objective.3, f32[16,512]{1,0:T(8,128)} %get-tuple-element.4.total_a, f32[16,1024]{1,0:T(8,128)} %get-tuple-element.5.total_b), custom_call_target="tpu_custom_call" | custom-call | tf_op jit(solution)/shard_map/choose/pallas_call | solution.py:730

commit v8 on v7

--- a/solution.py
+++ b/solution.py
@@ -56,7 +56,7 @@
 def whole_kernel(
     objective,
     scale,
-    attention,
+    attention_hbm,
     weight_hbm,
     residual_hbm,
     cotangent_hbm,
@@ -64,6 +64,7 @@
     up_hbm,
     out_a,
     out_b,
+    attention,
     middle,
     tokens,
     weight,
@@ -90,7 +91,6 @@
     from_x_b,
     slots_b,
     square_a,
-    from_x_a,
     slots_a,
     local,
     plane_send,
@@ -113,8 +113,7 @@
     stat_recv,
     bx_sems,
     bz_sems,
-    ax_sems,
-    az_sems,
+    a_sems,
 ):
     me_d = lax.axis_index("dp")
     me_t = lax.axis_index("tensor")
@@ -143,11 +142,15 @@
     def greet(device):
         pl.semaphore_signal(barrier, inc=1, device_id=device, device_id_type=MESH)
 
+    block = me_t // RING
+    own_place = lax.rem(me_t, RING)
+    for step in NEAR[:-1]:
+        greet(at_z(step + RING))
+    for step in (0, 4):
+        greet((me_d, (1 - block) * RING + lax.rem(own_place + step, RING)))
+    for step in range(1, RING):
+        greet((me_d, block * RING + lax.rem(own_place + step, RING)))
     greet(beside)
-    for step in range(1, GROUP):
-        greet((me_d, lax.rem(me_t + step, GROUP)))
-    for step in range(1, RING):
-        greet(at_z(step))
 
     def load(number):
         place = pl.ds(pl.multiple_of(me_t * features, features), features)
@@ -157,13 +160,14 @@
             (up_hbm, up),
             (residual_hbm, residual),
             (cotangent_hbm, cotangent),
+            (attention_hbm, attention),
         )
         return pltpu.make_async_copy(*pairs[number], local.at[number])
 
-    for number in range(5):
+    for number in (5, 0, 1, 2, 3, 4):
         load(number).start()
 
-    pl.semaphore_wait(barrier, 1 + GROUP - 1 + RING - 1)
+    pl.semaphore_wait(barrier, 2 * RING + 1)
 
     def piece(t):
         number = lax.rem(t // 4, 2) * 4 + lax.rem(t, 2) * 2 + lax.rem(t // 2, 2)
@@ -178,7 +182,7 @@
     def plane_copy(step, source):
         t = side * RING + lax.rem(me_t + step, RING)
         return remote(
-            attention.at[piece(t), :],
+            attention_hbm.at[piece(t), :],
             middle.at[source],
             plane_send.at[step],
             plane_recv.at[source],
@@ -195,9 +199,9 @@
             beside,
         )
 
-    own_place = lax.rem(me_t, RING)
     for step in range(1, RING):
         plane_copy(step, own_place).start()
+    load(5).wait()
     middle[own_place] = attention[piece(me_t), :]
 
     weight_copy(0, half).start()
@@ -435,6 +439,17 @@
     arrived(4)
     send_products(2, 0)
     send_products(2, 1)
+    for number in range(2, 5):
+        load(number).wait()
+    up_rows = up[...].reshape(ADAPTER_COUNT * ADAPTER_RANK, columns)
+    for step in range(PASSES):
+        up_wide[step] = lax.dot_general(
+            spread(objective[step], step),
+            up_rows,
+            (((0,), (0,)), ((), ())),
+            preferred_element_type=jnp.float32,
+        ).astype(jnp.bfloat16)
+    sums[...] = jnp.zeros(sums.shape, jnp.float32)
     weight_copy(2, 1 - half).wait_recv()
     weight_copy(3, 1 - half).wait_recv()
     send_products(4, 2)
@@ -449,24 +464,16 @@
     pass_on(7)
     send_products(3, 2)
     send_products(3, 3)
+    send_products(2, 2)
+    send_products(2, 3)
     low_end()
-    for number in range(2, 5):
-        load(number).wait()
-    up_rows = up[...].reshape(ADAPTER_COUNT * ADAPTER_RANK, columns)
     for step in range(PASSES):
-        choice = spread(objective[step], step)
         low_wide[step] = jnp.dot(
-            low_all[...], choice, preferred_element_type=jnp.float32
+            low_all[...], spread(objective[step], step), preferred_element_type=jnp.float32
         ).astype(jnp.bfloat16)
-        up_wide[step] = lax.dot_general(
-            choice, up_rows, (((0,), (0,)), ((), ())), preferred_element_type=jnp.float32
-        ).astype(jnp.bfloat16)
-    sums[...] = jnp.zeros(sums.shape, jnp.float32)
     arrived(7)
     own_products(0)
     own_products(1)
-    send_products(2, 2)
-    send_products(2, 3)
     send_products(1, 2)
     send_products(1, 3)
     own_products(2)
@@ -580,7 +587,16 @@
         return begin, middle, end, drain
 
     b_begin, b_middle, b_end, b_drain = owners(square_b, from_x_b, slots_b, bx_sems, bz_sems)
-    a_begin, a_middle, a_end, a_drain = owners(square_a, from_x_a, slots_a, ax_sems, az_sems)
+
+    def a_copy(step):
+        return remote(
+            square_a.at[lax.rem(me_d + step, GROUP)],
+            slots_a.at[step],
+            a_sems.at[0, step],
+            a_sems.at[1, step],
+            (lax.rem(me_d + step, GROUP), me_t),
+        )
+
     b_begin()
     back_middle()
     b_middle()
@@ -589,8 +605,7 @@
         back_all[...], attention[...], (((0,), (0,)), ((), ())), preferred_element_type=jnp.float32
     )
     square_a[...] = (per_a * per_a).astype(jnp.bfloat16).reshape(square_a.shape)
-    a_begin()
-    a_middle()
+    each_other(lambda step: a_copy(step).start())
     b_end(out_b)
 
     for step in range(1, RING):
@@ -614,8 +629,9 @@
 
     lax.fori_loop(0, chunks, ring_done, 0)
     b_drain()
-    a_end(out_a)
-    a_drain()
+    each_other(lambda step: a_copy(step).wait())
+    slots_a[0] = square_a[me_d]
+    out_a[...] = jnp.sum(slots_a[...].astype(jnp.float32), axis=0)
 
 
 def choose(objective, total, out):
@@ -662,9 +678,10 @@
             jax.ShapeDtypeStruct((share, features), f32),
             jax.ShapeDtypeStruct((share, columns), f32),
         ),
-        in_specs=[pl.BlockSpec(memory_space=pltpu.SMEM), vmem, vmem] + [hbm] * 5,
+        in_specs=[pl.BlockSpec(memory_space=pltpu.SMEM), vmem] + [hbm] * 6,
         out_specs=(vmem, vmem),
         scratch_shapes=[
+            pltpu.VMEM((LEN, features), bf16),
             pltpu.VMEM((RING, PIECE, features), bf16),
             pltpu.VMEM((RING, 2, LEN, features), bf16),
             pltpu.VMEM((2, depth, columns), bf16),
@@ -690,10 +707,9 @@
             pltpu.VMEM((2, RING, share, columns), bf16),
             pltpu.VMEM((RING, share, columns), bf16),
             pltpu.VMEM((RING, share, columns), bf16),
-            pltpu.VMEM((2, RING, share, features), bf16),
-            pltpu.VMEM((RING, share, features), bf16),
-            pltpu.VMEM((RING, share, features), bf16),
-            sem((5,)),
+            pltpu.VMEM((GROUP, share, features), bf16),
+            pltpu.VMEM((GROUP, share, features), bf16),
+            sem((6,)),
             sem((RING,)),
             sem((RING,)),
             sem((RING,)),
@@ -713,7 +729,8 @@
             sem((CHIPS,)),
             sem((CHIPS,)),
         ]
-        + [sem((2, RING))] * 4,
+        + [sem((2, RING))] * 2
+        + [sem((2, GROUP))],
         compiler_params=pltpu.CompilerParams(
             collective_id=0, has_side_effects=True, vmem_limit_bytes=56 * 2**20
         ),

time: 114 us -> 114 us (level)
  no operation moved by 1% of the time
where the time goes in v8:
time: 114 us
  Pallas kernels  113 us (99%)
    pallas_call x1, Pallas kernels, body(): pl.pallas_call(whole_kernel, name='fisher', out_shape=(jax.ShapeDtypeStru...  111 us

profile of v8, /device:TPU:1, one launch (start us, length us, event | category | flops | bytes accessed | tf_op | source)
XLA Modules:
  0.0 113.6 jit_solution(14076886346623006664)
XLA Ops:
  0.6 111.4 %fisher.1 = (f32[16,512]{1,0:T(8,128)}, f32[16,1024]{1,0:T(8,128)}) custom-call(s32[4]{0:T(128)} %objective.3, f32[1,1024]{1,0:T(1,128)} %bitcast.1, bf16[256,512]{1,0:T(8,128)(2,1)} %attention_hbm.1, bf16[512,1024]{1,0:T(8,128)(2,1)} %weight_hbm.1, bf16[256,1024]{1,0:T(8,128)(2,1)} %residual_hbm.1, bf16[4,256,1024]{2,1,0:T(8,128)(2,1)} %cotangent_hbm.1, ...), custom_call_target="tpu_custom_call" | custom-call | tf_op jit(solution)/shard_map/fisher/pallas_call | solution.py:674
  112.0 1.6 %choose.1 = (f32[4,4,512]{2,1,0:T(4,128)}, f32[4,4,1024]{2,1,0:T(4,128)}) custom-call(s32[4]{0:T(128)} %objective.3, f32[16,512]{1,0:T(8,128)} %get-tuple-element.4.total_a, f32[16,1024]{1,0:T(8,128)} %get-tuple-element.5.total_b), custom_call_target="tpu_custom_call" | custom-call | tf_op jit(solution)/shard_map/choose/pallas_call | solution.py:747

commit v9 on v8

--- a/solution.py
+++ b/solution.py
@@ -369,15 +369,18 @@
 
     def own_products(chunk):
         cols = cols_of(chunk)
-        value = product(NEAR.index(0), cols)
+        value = product(NEAR.index(0), cols) + residual[:, cols].astype(jnp.float32)
+        for step in range(PASSES):
+            hidden[step, :, cols] = value + jnp.dot(
+                low_wide[step], up_wide[step, :, cols], preferred_element_type=jnp.float32
+            )
         for way in range(2):
             ring_copy(way, 1, chunk).wait_recv()
-            value = value + ring_in[way, 0, chunk].astype(jnp.float32)
-        value = value + residual[:, cols].astype(jnp.float32)
+        arrived_sum = ring_in[0, 0, chunk].astype(jnp.float32) + ring_in[1, 0, chunk].astype(
+            jnp.float32
+        )
         for step in range(PASSES):
-            here = value + jnp.dot(
-                low_wide[step], up_wide[step, :, cols], preferred_element_type=jnp.float32
-            )
+            here = hidden[step, :, cols] + arrived_sum
             hidden[step, :, cols] = here
             weighted = cotangent[step, :, cols].astype(jnp.float32) * scale[:, cols]
             squares = here * here

time: 114 us -> 114 us (level)
  no operation moved by 1% of the time
where the time goes in v9:
time: 114 us
  Pallas kernels  113 us (99%)
    pallas_call x1, Pallas kernels, body(): pl.pallas_call(whole_kernel, name='fisher', out_shape=(jax.ShapeDtypeStru...  112 us

profile of v9, /device:TPU:1, one launch (start us, length us, event | category | flops | bytes accessed | tf_op | source)
XLA Modules:
  0.0 114.0 jit_solution(6417908164188271168)
XLA Ops:
  0.6 111.8 %fisher.1 = (f32[16,512]{1,0:T(8,128)}, f32[16,1024]{1,0:T(8,128)}) custom-call(s32[4]{0:T(128)} %objective.3, f32[1,1024]{1,0:T(1,128)} %bitcast.1, bf16[256,512]{1,0:T(8,128)(2,1)} %attention_hbm.1, bf16[512,1024]{1,0:T(8,128)(2,1)} %weight_hbm.1, bf16[256,1024]{1,0:T(8,128)(2,1)} %residual_hbm.1, bf16[4,256,1024]{2,1,0:T(8,128)(2,1)} %cotangent_hbm.1, ...), custom_call_target="tpu_custom_call" | custom-call | tf_op jit(solution)/shard_map/fisher/pallas_call | solution.py:677
  112.4 1.6 %choose.1 = (f32[4,4,512]{2,1,0:T(4,128)}, f32[4,4,1024]{2,1,0:T(4,128)}) custom-call(s32[4]{0:T(128)} %objective.3, f32[16,512]{1,0:T(8,128)} %get-tuple-element.4.total_a, f32[16,1024]{1,0:T(8,128)} %get-tuple-element.5.total_b), custom_call_target="tpu_custom_call" | custom-call | tf_op jit(solution)/shard_map/choose/pallas_call | solution.py:750
